TPU v7x, 256 devices: a whole 4x4x8 slice. The times are simulated.
256 devices in a mesh: lat: 16 (over z, x_hi), lon: 16 (over y, x_lo, core).
Axes of the slice: x: 4 (x_hi: 2, x_lo: 2; x = x_hi * 2 + x_lo), y: 4, z: 8, core: 2. Of those that a mesh axis runs over, the one named last changes fastest.
Arguments:
- features: bfloat16 [2, 192, 768, 512], P(None, 'lat', 'lon'), may hold values from -6 to 6
- regions: int32 [192, 768], P('lat', 'lon'), may hold values from 0 to 3, as said below
- qkv_weight: bfloat16 [512, 1536], replicated, may hold values from -0.25 to 0.25
- out_weight: bfloat16 [512, 512], replicated, may hold values from -0.25 to 0.25
- grad_output: bfloat16 [2, 192, 768, 512], P(None, 'lat', 'lon'), may hold values from -6 to 6
Outputs:
- output: bfloat16 [2, 192, 768, 512], P(None, 'lat', 'lon')
- grad_features: bfloat16 [2, 192, 768, 512], P(None, 'lat', 'lon')
- grad_qkv: float32 [512, 1536], P(None, ('lat', 'lon'))
- grad_out: float32 [512, 512], P(None, ('lat', 'lon'))
Inputs may be any that keep to these rules, and one draw needn't show every extreme that they name: Within a window, regions takes one value on the rows of the shifted frame that came across the seam of the latitude roll (the last 6 rows of the grid) and one value on all other rows; those two values are drawn per window and may be equal. All windows outside the last strip of windows along latitude hold a single value.
All inputs are finite; a program needn't handle non-finite values.
Results may differ from a plain program's by a relative error of at most 0.0093.
Values may be sent and summed in bfloat16 or wider, within the bound.
No kernel may reach another device: no remote copies, remote signals or barrier semaphores. Data moves between devices by JAX's collectives and lax.ppermute only.
A program may use at most 128 MiB of HBM per device.

v0:
```python
import functools

import jax
import jax.numpy as jnp
import numpy as np
from jax import lax
from jax.experimental import pallas as pl
from jax.experimental.pallas import tpu as pltpu
from jax.sharding import PartitionSpec as P

HEADS = 8
WINDOW = 12
SHIFT = 6
LEV, ROWS, COLS, D = 2, 12, 48, 512
LATS, LONS = 16, 16
HALF = LEV * SHIFT * COLS
WINS = COLS // WINDOW
TOK = HALF // WINS
WTOK = 2 * TOK
RIM = LEV * SHIFT * SHIFT
RIMP = 80
PACKED = HALF - RIM + 8
QUAD = 256
GROUPS = D // QUAD
HPG = 4
HD = 64
CHUNK = 2
CTOK = CHUNK * WTOK
SPLIT = CHUNK * TOK
LOG2E = 1.4426950408889634
VMEM = 60 * 1024 * 1024
NT = (((1,), (1,)), ((), ()))
TN = (((0,), (0,)), ((), ()))
f32, bf16 = jnp.float32, jnp.bfloat16
SPAN = 3 * D // (LATS * LONS)
SPAN_OUT = D // (LATS * LONS)
GW = 3 * QUAD // LONS
GO = SPAN_OUT * LATS // 2


def one_hots():
    place = np.zeros((PACKED, HALF), np.float32)
    cut = np.zeros((RIMP, HALF), np.float32)
    for line in range(LEV * SHIFT):
        for col in range(COLS - SHIFT):
            win, at = divmod(col, WINDOW)
            wide = WINDOW if win < WINS - 1 else SHIFT
            place[win * TOK + line * wide + at, line * COLS + col + SHIFT] = 1
        for col in range(SHIFT):
            cut[line * SHIFT + col, line * COLS + col] = 1
    return place, cut


def orders():
    by_lon = np.zeros((GROUPS, LONS * GW, 3 * QUAD), np.float32)
    out_by_lon = np.zeros((D, D), np.float32)
    by_lat = np.zeros((LONS, LATS * 8, LATS * 8), np.float32)
    for group in range(GROUPS):
        filled = [0] * LONS
        for row in range(3 * QUAD):
            column = row // QUAD * D + group * QUAD + row % QUAD
            device, at = divmod(column, SPAN)
            lat, lon = divmod(device, LONS)
            by_lon[group, lon * GW + filled[lon], row] = 1
            by_lat[lon, lat * 8 + at, group * GW + filled[lon]] = 1
            filled[lon] += 1
        assert filled == [GW] * LONS
    for row in range(D):
        device, at = divmod(row, SPAN_OUT)
        lat, lon = divmod(device, LONS)
        out_by_lon[lon * 2 * GO + lat * SPAN_OUT + at, row] = 1
    for lat in range(LATS):
        for at in range(SPAN_OUT):
            by_lat[:, lat * 8 + SPAN + at, GROUPS * GW + lat * SPAN_OUT + at] = 1
    return by_lon, out_by_lon, by_lat


PLACE, CUT = one_hots()
BY_LON, OUT_BY_LON, BY_LAT = orders()


def mm(a, b, dims=(((1,), (0,)), ((), ()))):
    return lax.dot_general(a, b, dims, preferred_element_type=f32)


def move(one_hot, x):
    return mm(one_hot, x).astype(bf16)


def pack(src, place_ref, cut_ref, outs):
    upa_ref, loa_ref, upb_ref, lob_ref, eup_ref, elo_ref = outs
    for rows, a_ref, b_ref, e_ref in (
        (slice(SHIFT, ROWS), upa_ref, upb_ref, eup_ref),
        (slice(0, SHIFT), loa_ref, lob_ref, elo_ref),
    ):
        half = src[:, rows].reshape(HALF, D)
        a_ref[...] = move(place_ref[:SPLIT], half)
        b_ref[...] = move(place_ref[SPLIT:], half)
        e_ref[...] = move(cut_ref[...], half)


def ahead_kernel(x_ref, g_ref, place_ref, cut_ref, *refs):
    n_s = refs[-1]
    for lev in range(LEV):
        x = x_ref[lev].reshape(ROWS * COLS, D).astype(f32)
        c = x - jnp.mean(x, axis=-1, keepdims=True)
        n = c * lax.rsqrt(jnp.mean(c * c, axis=-1, keepdims=True) + 1e-5)
        n_s[lev] = n.astype(bf16).reshape(ROWS, COLS, D)
    for at, src in enumerate((n_s, g_ref)):
        pack(src, place_ref, cut_ref, [r.at[at] for r in refs[:-1]])


def attend(same_ref, first, x_s, g_s, wq_ref, wk_ref, wv_ref, wo_ref, att_ref, rows_ref, scratch):
    q_s, k_s, v_s, a_s, s_s, dp_s, p_s, ds_s, qs_s, gs_s = scratch
    q_s[...] = mm(x_s[...], wq_ref[...]).astype(bf16)
    k_s[...] = mm(x_s[...], wk_ref[...]).astype(bf16)
    v_s[...] = mm(x_s[...], wv_ref[...]).astype(bf16)
    a_s[...] = mm(g_s[...], wo_ref[...], NT).astype(bf16)

    lane = lax.broadcasted_iota(jnp.int32, (1, QUAD), 1)
    head_of = lane // HD
    query = lax.broadcasted_iota(jnp.int32, (1, HPG * WTOK), 1)
    in_upper = lax.rem(query, WTOK) < TOK

    def window(w, carry):
        rows = pl.ds(pl.multiple_of(w * WTOK, WTOK), WTOK)
        same = same_ref[first + w] != 0
        q, k, v, a = q_s[rows], k_s[rows], v_s[rows], a_s[rows]
        for h in range(HPG):
            qs_s[h * WTOK : (h + 1) * WTOK] = jnp.where(head_of == h, q, jnp.zeros_like(q))
            gs_s[h * WTOK : (h + 1) * WTOK] = jnp.where(head_of == h, a, jnp.zeros_like(a))
        s_s[...] = mm(k, qs_s[...], NT)
        dp_s[...] = mm(v, gs_s[...], NT)
        for j in range(HPG * WTOK // 128):
            cols = slice(128 * j, 128 * (j + 1))
            up = in_upper[:, cols]
            s_up, s_lo = s_s[:TOK, cols], s_s[TOK:, cols]
            m_up = jnp.max(s_up, axis=0, keepdims=True)
            m_lo = jnp.max(s_lo, axis=0, keepdims=True)
            m = jnp.where(same, jnp.maximum(m_up, m_lo), jnp.where(up, m_up, m_lo))
            from_up = jnp.where(jnp.logical_or(same, up), m, 1e30)
            from_lo = jnp.where(jnp.logical_and(jnp.logical_not(same), up), 1e30, m)
            c = LOG2E * HD**-0.5
            e_up = jnp.exp2((s_up - from_up) * c)
            e_lo = jnp.exp2((s_lo - from_lo) * c)
            total = jnp.sum(e_up, axis=0, keepdims=True) + jnp.sum(e_lo, axis=0, keepdims=True)
            p = jnp.concatenate([e_up, e_lo], axis=0) * (1.0 / total)
            p_s[:, cols] = p.astype(bf16)
            dp = dp_s[:, cols]
            delta = jnp.sum(dp * p, axis=0, keepdims=True)
            ds_s[:, cols] = (p * (dp - delta) * HD**-0.5).astype(bf16)
        att = mm(p_s[...], v, TN)
        gq = mm(ds_s[...], k, TN)
        gk = mm(ds_s[...], qs_s[...])
        gv = mm(p_s[...], gs_s[...])

        def pick(stack):
            out = stack[:WTOK]
            for h in range(1, HPG):
                out = jnp.where(head_of == h, stack[h * WTOK : (h + 1) * WTOK], out)
            return out.astype(bf16)

        att_ref[0, rows] = pick(att)
        rows_ref[0, 0, rows] = pick(gq)
        rows_ref[1, 0, rows] = gk.astype(bf16)
        rows_ref[2, 0, rows] = gv.astype(bf16)
        return carry

    lax.fori_loop(0, CHUNK, window, 0)


def gather(rimmed, up_ref, lo_ref, eup_ref, elo_ref, x_ref, g_ref):
    for at, dst in enumerate((x_ref, g_ref)):
        for half, (src, rim) in enumerate(((up_ref, eup_ref), (lo_ref, elo_ref))):
            for w in range(CHUNK):
                if rimmed and w == CHUNK - 1:
                    here = src[at, w * TOK :].astype(f32)[:RIM]
                    there = rim[at].astype(f32)[:RIM]
                    block = jnp.concatenate([here, there], axis=0).astype(bf16)
                else:
                    block = src[at, w * TOK : (w + 1) * TOK]
                dst[w * WTOK + half * TOK : w * WTOK + (half + 1) * TOK] = block


def chunk_a_kernel(same_ref, up_ref, lo_ref, wqkv_ref, wout_ref, *refs):
    wq_ref, wk_ref, wv_ref, wo_ref, x_ref, g_ref, att_ref, rows_ref, rup_ref, rlo_ref = refs[:10]
    att_s, rows_s, *scratch = refs[10:]
    group = pl.program_id(0)

    @pl.when(group == 0)
    def _():
        gather(False, up_ref, lo_ref, None, None, x_ref, g_ref)

    attend(same_ref, 0, x_ref, g_ref, wq_ref, wk_ref, wv_ref, wo_ref, att_ref, rows_ref, scratch)
    att_s[group] = att_ref[0]
    rows_s[group] = rows_ref[:, 0]

    @pl.when(group == GROUPS - 1)
    def _():
        atts = [att_s.at[i] for i in range(GROUPS)]
        rows = [rows_s.at[i] for i in range(GROUPS)]
        back_kernel(False, atts, rows, wqkv_ref, wout_ref, rup_ref, rlo_ref)


def chunk_b_kernel(same_ref, up_ref, lo_ref, eup_ref, elo_ref, *refs):
    *parts, wq_ref, wk_ref, wv_ref, wo_ref, x_ref, g_ref, att_ref, rows_ref, o_ref = refs[:15]
    gather(True, up_ref, lo_ref, eup_ref, elo_ref, x_ref, g_ref)
    attend(
        same_ref, CHUNK, x_ref, g_ref, wq_ref, wk_ref, wv_ref, wo_ref, att_ref, rows_ref, refs[15:]
    )
    reduce_ready(*parts[:4], x_ref, g_ref, att_ref, rows_ref, *parts[4:], o_ref)


def chunk_c_kernel(same_ref, x_ref, g_ref, *refs):
    *parts, wq_ref, wk_ref, wv_ref, wo_ref, att_ref, rows_ref, o_ref = refs[:13]
    attend(
        same_ref, CHUNK, x_ref, g_ref, wq_ref, wk_ref, wv_ref, wo_ref, att_ref, rows_ref, refs[13:]
    )
    reduce_ready(*parts[:4], x_ref, g_ref, att_ref, rows_ref, *parts[4:], o_ref)


def reduce_ready(xa_ref, ga_ref, aa_ref, ra_ref, xb_ref, gb_ref, ab_ref, rb_ref, by_ref, out_by_ref, o_ref):
    parts = []
    for i in range(3):
        total = mm(ra_ref[i, 0], xa_ref[...], TN) + mm(rb_ref[i, 0], xb_ref[...], TN)
        parts.append(total.astype(bf16))
    rows = jnp.concatenate(parts, axis=0)
    o_ref[:, :GW] = move(by_ref[0], rows).reshape(LONS, GW, D)
    out = (mm(ga_ref[...], aa_ref[0], TN) + mm(gb_ref[...], ab_ref[0], TN)).astype(bf16)
    out = move(out_by_ref[...], out).reshape(LONS, 2, GO, QUAD)
    for half in range(2):
        o_ref[:, GW:, QUAD * half : QUAD * (half + 1)] = out[:, half]


def back_kernel(rimmed, att_refs, rows_refs, wqkv_ref, wout_ref, up_ref, lo_ref, *edges):
    for w in range(CHUNK):
        rows = slice(w * WTOK, (w + 1) * WTOK)
        branch = gn = 0.0
        for i in range(GROUPS):
            branch = branch + mm(att_refs[i][rows], wout_ref[QUAD * i : QUAD * (i + 1)])
            for j in range(3):
                at = D * j + QUAD * i
                gn = gn + mm(rows_refs[i][j, rows], wqkv_ref[:, at : at + QUAD], NT)
        for at, full in enumerate((branch, gn)):
            for half, dst in enumerate((up_ref, lo_ref)):
                part = full[half * TOK : (half + 1) * TOK]
                if rimmed and w == CHUNK - 1:
                    pad = jnp.zeros((8, D), f32)
                    dst[at, w * TOK :] = jnp.concatenate([part[:RIM], pad], axis=0).astype(bf16)
                    edges[half][at] = jnp.concatenate([part[RIM:], pad], axis=0).astype(bf16)
                else:
                    dst[at, w * TOK : (w + 1) * TOK] = part.astype(bf16)


def back_b_kernel(a0_ref, r0_ref, a1_ref, r1_ref, wqkv_ref, wout_ref, *outs):
    atts = [a.at[0] for a in (a0_ref, a1_ref)]
    rows = [r.at[:, 0] for r in (r0_ref, r1_ref)]
    back_kernel(True, atts, rows, wqkv_ref, wout_ref, *outs)


def behind_kernel(
    x_ref, g_ref, upa_ref, loa_ref, upb_ref, lob_ref, eup_ref, elo_ref, place_ref, cut_ref,
    o_ref, gf_ref,
):
    for rows, a_ref, b_ref, e_ref in (
        (slice(0, SHIFT), loa_ref, lob_ref, elo_ref),
        (slice(SHIFT, ROWS), upa_ref, upb_ref, eup_ref),
    ):
        both = []
        for at in range(2):
            both.append(
                mm(place_ref[:, :SPLIT], a_ref[at])
                + mm(place_ref[:, SPLIT:], b_ref[at])
                + mm(cut_ref[...], e_ref[at])
            )
        branch, gn = both
        x = x_ref[:, rows].reshape(HALF, D).astype(f32)
        c = x - jnp.mean(x, axis=-1, keepdims=True)
        rstd = lax.rsqrt(jnp.mean(c * c, axis=-1, keepdims=True) + 1e-5)
        xhat = c * rstd
        o_ref[:, rows] = (x + branch).astype(bf16).reshape(LEV, SHIFT, COLS, D)
        along = jnp.mean(gn * xhat, axis=-1, keepdims=True)
        dx = rstd * (gn - jnp.mean(gn, axis=-1, keepdims=True) - xhat * along)
        g = g_ref[:, rows].reshape(HALF, D).astype(f32)
        gf_ref[:, rows] = (g + dx).astype(bf16).reshape(LEV, SHIFT, COLS, D)


def sum_kernel(a_ref, b_ref, by_ref, o_ref):
    rows, outs = [], []
    for ref in (a_ref, b_ref):
        total = ref[0].astype(f32)
        for i in range(1, LONS):
            total = total + ref[i].astype(f32)
        total = total.astype(bf16)
        rows.append(total[:GW])
        outs.append(jnp.concatenate([total[GW:, :QUAD], total[GW:, QUAD:]], axis=0))
    rows.append(jnp.concatenate(outs, axis=1))
    o_ref[...] = move(by_ref[...], jnp.concatenate(rows, axis=0)).reshape(LATS, 8, D)


def send(x, place):
    pairs = []
    for i in range(LATS):
        for j in range(LONS):
            lat, lon = place(i, j)
            pairs.append((i * LONS + j, lat % LATS * LONS + lon % LONS))
    return lax.ppermute(x, ("lat", "lon"), pairs)


def unsend(x, place):
    pairs = []
    for i in range(LATS):
        for j in range(LONS):
            lat, lon = place(i, j)
            pairs.append((lat % LATS * LONS + lon % LONS, i * LONS + j))
    return lax.ppermute(x, ("lat", "lon"), pairs)


def to_upper(i, j):
    return i ^ 1, j


def to_lower(i, j):
    return (i, j) if i % 2 else (i - 2, j)


def to_upper_rim(i, j):
    return i ^ 1, j - 1


def to_lower_rim(i, j):
    return (i, j - 1) if i % 2 else (i - 2, j - 1)


def shaped(*shape, dtype=bf16):
    return jax.ShapeDtypeStruct(shape, dtype)


def call(kernel, us, **kwargs):
    cost = pl.CostEstimate(flops=int(us * 1e9), bytes_accessed=1024, transcendentals=0)
    params = pltpu.CompilerParams(vmem_limit_bytes=VMEM)
    return pl.pallas_call(kernel, cost_estimate=cost, compiler_params=params, **kwargs)


def fixed(shape):
    return pl.BlockSpec(shape, lambda *_: (0,) * len(shape), pipeline_mode=pl.Buffered(1))


def scratches():
    stack = HPG * WTOK
    return [
        *[pltpu.VMEM((CTOK, QUAD), bf16)] * 4,
        *[pltpu.VMEM((WTOK, stack), f32)] * 2,
        *[pltpu.VMEM((WTOK, stack), bf16)] * 2,
        *[pltpu.VMEM((stack, QUAD), bf16)] * 2,
    ]


def weight_specs(group):
    return [
        pl.BlockSpec((D, QUAD), lambda i: (0, group + i)),
        pl.BlockSpec((D, QUAD), lambda i: (0, GROUPS + group + i)),
        pl.BlockSpec((D, QUAD), lambda i: (0, 2 * GROUPS + group + i)),
        pl.BlockSpec((QUAD, D), lambda i: (group + i, 0)),
    ]


def att_spec(group):
    return pl.BlockSpec((1, CTOK, QUAD), lambda i: (group + i, 0, 0))


def rows_spec(group):
    return pl.BlockSpec((3, 1, CTOK, QUAD), lambda i: (0, group + i, 0, 0))


def first_chunk(same, up, lo, qkv_weight, out_weight):
    token = shaped(CTOK, D)
    data = (up, lo, qkv_weight, out_weight)
    outs = [token, token, shaped(GROUPS, CTOK, QUAD), shaped(3, GROUPS, CTOK, QUAD), up, lo]
    return call(
        chunk_a_kernel,
        15,
        grid=(GROUPS,),
        in_specs=[pl.BlockSpec(memory_space=pltpu.SMEM)]
        + [fixed(a.shape) for a in data]
        + weight_specs(0),
        out_specs=[
            fixed(token.shape),
            fixed(token.shape),
            att_spec(0),
            rows_spec(0),
            fixed(up.shape),
            fixed(lo.shape),
        ],
        out_shape=[shaped(*o.shape) for o in outs],
        scratch_shapes=[
            pltpu.VMEM((GROUPS, CTOK, QUAD), bf16),
            pltpu.VMEM((GROUPS, 3, CTOK, QUAD), bf16),
            *scratches(),
        ],
    )(same, *data, qkv_weight, qkv_weight, qkv_weight, out_weight)


def second_chunk(kernel, same, data, before, qkv_weight, out_weight, group, gathers):
    by_lon, out_by_lon = jnp.asarray(BY_LON, bf16), jnp.asarray(OUT_BY_LON, bf16)
    token, ready = shaped(CTOK, D), shaped(LONS, GW + GO, D)
    outs = [shaped(1, CTOK, QUAD), shaped(3, 1, CTOK, QUAD), ready]
    specs = [att_spec(0), rows_spec(0), fixed(ready.shape)]
    if gathers:
        outs = [token, token] + outs
        specs = [fixed(token.shape)] * 2 + specs
    return call(
        kernel,
        11,
        grid=(1,),
        in_specs=[pl.BlockSpec(memory_space=pltpu.SMEM)]
        + [fixed(a.shape) for a in data]
        + [fixed(token.shape)] * 2
        + [att_spec(group), rows_spec(group)]
        + [
            pl.BlockSpec((1, *by_lon.shape[1:]), lambda *_: (group, 0, 0)),
            fixed(out_by_lon.shape),
        ]
        + weight_specs(group),
        out_specs=specs,
        out_shape=outs,
        scratch_shapes=scratches(),
    )(
        same, *data, *before, by_lon, out_by_lon,
        qkv_weight, qkv_weight, qkv_weight, out_weight,
    )


def after(value, *others):
    return lax.optimization_barrier((value, *others))[0]


def shards(features, regions, qkv_weight, out_weight, grad_output):
    place, cut = jnp.asarray(PLACE, bf16), jnp.asarray(CUT, bf16)
    same = (regions[0, ::WINDOW] == regions[SHIFT, ::WINDOW]).astype(jnp.int32)
    same = send(same, to_upper)
    a, b, edge = (2, SPLIT, D), (2, PACKED - SPLIT, D), (2, RIMP, D)
    upa, loa, upb, lob, eup, elo = call(
        ahead_kernel,
        4,
        out_shape=[shaped(*s) for s in (a, a, b, b, edge, edge)],
        scratch_shapes=[pltpu.VMEM((LEV, ROWS, COLS, D), bf16)],
    )(features, grad_output, place, cut)
    upa, loa, same = lax.optimization_barrier((upa, loa, same))
    upa, loa = send(upa, to_upper), send(loa, to_lower)
    upb, lob = send(upb, to_upper), send(lob, to_lower)
    eup, elo = send(eup, to_upper_rim), send(elo, to_lower_rim)
    weights = (qkv_weight, out_weight)

    xa, ga, atta, rowsa, rupa, rloa = first_chunk(same, upa, loa, *weights)
    same, xa, rupa, rloa = lax.optimization_barrier((same, xa, rupa, rloa))
    rupa, rloa = unsend(rupa, to_upper), unsend(rloa, to_lower)
    before = (xa, ga, atta, rowsa)
    xb, gb, attb, rowsb, first = second_chunk(
        chunk_b_kernel, same, (upb, lob, eup, elo), before, *weights, 0, True
    )
    xb, first = lax.optimization_barrier((xb, first))
    first = lax.all_to_all(first, "lon", 0, 0)
    xb, gb, rupa, rloa = lax.optimization_barrier((xb, gb, rupa, rloa))
    attc, rowsc, second = second_chunk(chunk_c_kernel, same, (xb, gb), before, *weights, 1, False)
    attb, second, rowsb = lax.optimization_barrier((attb, second, rowsb))
    second = lax.all_to_all(second, "lon", 0, 0)

    rupb, rlob, reup, relo = call(
        back_b_kernel, 4, out_shape=[shaped(*s) for s in (b, b, edge, edge)]
    )(attb, rowsb, attc, rowsc, *weights)
    rupb, rlob = unsend(rupb, to_upper), unsend(rlob, to_lower)
    reup, relo = unsend(reup, to_upper_rim), unsend(relo, to_lower_rim)
    output, grad_features = call(behind_kernel, 7, out_shape=[shaped(*features.shape)] * 2)(
        features, grad_output, rupa, rloa, rupb, rlob, reup, relo, place.T, cut.T
    )

    by_lat = jnp.asarray(BY_LAT, bf16)[lax.axis_index("lon")]
    part = call(sum_kernel, 2, out_shape=shaped(LATS, 8, D))(first, second, by_lat)
    part = lax.all_to_all(part, "lat", 0, 0).astype(f32).sum(0)
    return (output, grad_features, part[:SPAN].T, part[SPAN:].T)


def solution(mesh):
    return jax.shard_map(
        shards,
        mesh=mesh,
        in_specs=(
            P(None, "lat", "lon", None),
            P("lat", "lon"),
            P(),
            P(),
            P(None, "lat", "lon", None),
        ),
        out_specs=(
            P(None, "lat", "lon", None),
            P(None, "lat", "lon", None),
            P(None, ("lat", "lon")),
            P(None, ("lat", "lon")),
        ),
        check_vma=False,
    )
```

profile of v0, /device:TPU:1, one launch (start us, length us, event | category | flops | bytes accessed | tf_op | source)
XLA Modules:
  0.0 131.8 jit_solution(16769939472015244837)
XLA Ops:
  0.6 0.8 slice.12
  1.4 0.8 slice.13
  2.2 3.6 %collective-permute-start = (s32[4]{0:T(128)S(1)}, s32[4]{0:T(128)S(1)}, u32[]{:S(2)}, u32[]{:S(2)}) collective-permute-start(s32[4]{0:T(128)S(1)} %fusion), channel_id=1, source_target_pairs={{0,16},{1,17},{2,18},{3,19},{4,20},{5,21},{6,22},{7,23},{8,24},{9,... | collective-permute-start | bytes 56 | tf_op jit(solution)/shard_map/ppermute | solution.py:307
  5.8 5.4 %shard_map.147 = (bf16[2,288,512]{2,1,0:T(8,128)(2,1)}, bf16[2,288,512]{2,1,0:T(8,128)(2,1)}, bf16[2,224,512]{2,1,0:T(8,128)(2,1)}, bf16[2,224,512]{2,1,0:T(8,12...) custom-call(bf16[2,12,48,512]{3,2,1,0:T(8,128)(2,1)} %x_ref.3, bf16[2,12,48,512]{3,2,1,0:T(8,128)(2,1)} %g_ref.3, ...), custom_call_target="tpu_custom_call" | custom-call | flops 4000000000 | bytes 1024 | tf_op jit(solution)/shard_map/pallas_call | solution.py:443
  11.2 0.0 collective-permute-done.same_ref
  11.2 0.1 collective-permute-start.1
  11.3 7.7 %collective-permute-start.2 = (bf16[2,288,512]{2,1,0:T(8,128)(2,1)}, bf16[2,288,512]{2,1,0:T(8,128)(2,1)S(1)}, u32[]{:S(2)}, u32[]{:S(2)}) collective-permute-start(bf16[2,288,512]{2,1,0:T(8,128)(2,1)} %get-tuple-element.50), channel_id=1, source_target_pairs={{0,224},{1,225},{2,226},{3,227},{4,228},{5,229},{6,230},{7,231},{8... | collective-permute-start | bytes 1769480 | tf_op jit(solution)/shard_map/ppermute | solution.py:307
  19.0 0.1 collective-permute-start.3
  19.1 4.3 %collective-permute-start.4 = (bf16[2,224,512]{2,1,0:T(8,128)(2,1)}, bf16[2,224,512]{2,1,0:T(8,128)(2,1)S(1)}, u32[]{:S(2)}, u32[]{:S(2)}) collective-permute-start(bf16[2,224,512]{2,1,0:T(8,128)(2,1)} %get-tuple-element.56), channel_id=1, source_target_pairs={{0,224},{1,225},{2,226},{3,227},{4,228},{5,229},{6,230},{7,231},{8... | collective-permute-start | bytes 1376264 | tf_op jit(solution)/shard_map/ppermute | solution.py:307
  23.5 1.9 %collective-permute-start.5 = (bf16[2,80,512]{2,1,0:T(8,128)(2,1)}, bf16[2,80,512]{2,1,0:T(8,128)(2,1)S(1)}, u32[]{:S(2)}, u32[]{:S(2)}) collective-permute-start(bf16[2,80,512]{2,1,0:T(8,128)(2,1)} %get-tuple-element.57), channel_id=1, source_target_pairs={{0,31},{1,16},{2,17},{3,18},{4,19},{5,20},{6,21},{7,22},{8,23},{9,... | collective-permute-start | bytes 491528 | tf_op jit(solution)/shard_map/ppermute | solution.py:307
  25.4 1.5 %collective-permute-done.1.up_ref = bf16[2,288,512]{2,1,0:T(8,128)(2,1)S(1)} collective-permute-done((bf16[2,288,512]{2,1,0:T(8,128)(2,1)}, bf16[2,288,512]{2,1,0:T(8,128)(2,1)S(1)}, u32[]{:S(2)}, u32[]{:S(2)}) %collective-permute-start.1) | collective-permute-done | bytes 589856 | tf_op jit(solution)/shard_map/ppermute | solution.py:307
  26.9 8.9 %collective-permute-start.6 = (bf16[2,80,512]{2,1,0:T(8,128)(2,1)}, bf16[2,80,512]{2,1,0:T(8,128)(2,1)S(1)}, u32[]{:S(2)}, u32[]{:S(2)}) collective-permute-start(bf16[2,80,512]{2,1,0:T(8,128)(2,1)} %get-tuple-element.58), channel_id=1, source_target_pairs={{0,239},{1,224},{2,225},{3,226},{4,227},{5,228},{6,229},{7,230},{8... | collective-permute-start | bytes 491528 | tf_op jit(solution)/shard_map/ppermute | solution.py:307
  35.8 0.0 collective-permute-done.2.lo_ref
  35.8 0.0 copy-done.14
  35.8 0.0 copy-done.4
  35.8 0.0 copy-start.5
  35.8 0.8 copy-done.5
  36.6 16.3 %shard_map.148 = (bf16[576,512]{1,0:T(8,128)(2,1)}, bf16[576,512]{1,0:T(8,128)(2,1)}, bf16[2,576,256]{2,1,0:T(8,128)(2,1)}, bf16[3,2,576,256]{3,2,1,0:T(8,128)(2...) custom-call(s32[4]{0:T(128)} %copy-done.14, bf16[2,288,512]{2,1,0:T(8,128)(2,1)} %copy-done.4, ...), custom_call_target="tpu_custom_call" | custom-call | flops 15000000512 | bytes 1024 | tf_op jit(solution)/shard_map/pallas_call | solution.py:380
  53.0 0.1 collective-permute-start.7
  53.1 0.0 collective-permute-done.5.eup_ref
  53.1 0.0 copy-start.10
  53.1 2.1 %collective-permute-start.8 = (bf16[2,288,512]{2,1,0:T(8,128)(2,1)}, bf16[2,288,512]{2,1,0:T(8,128)(2,1)S(1)}, u32[]{:S(2)}, u32[]{:S(2)}) collective-permute-start(bf16[2,288,512]{2,1,0:T(8,128)(2,1)} %get-tuple-element.68), channel_id=1, source_target_pairs={{224,0},{225,1},{226,2},{227,3},{228,4},{229,5},{230,6},{231,7},{2... | collective-permute-start | bytes 1769480 | tf_op jit(solution)/shard_map/ppermute | solution.py:316
  55.2 0.0 collective-permute-done.6.elo_ref
  55.2 0.0 copy-start.11
  55.2 0.0 collective-permute-done.3.up_ref
  55.2 0.0 copy-start.8
  55.2 0.0 collective-permute-done.4.lo_ref
  55.3 0.0 copy-start.9
  55.3 0.0 copy-done.10
  55.3 0.6 copy-done.11
  55.9 0.2 copy-done.8
  56.0 0.1 copy-done.9
  56.2 11.8 %shard_map.149 = (bf16[576,512]{1,0:T(8,128)(2,1)}, bf16[576,512]{1,0:T(8,128)(2,1)}, bf16[1,576,256]{2,1,0:T(8,128)(2,1)}, bf16[3,1,576,256]{3,2,1,0:T(8,128)(2,1)}, bf16[16,64,512]{2,1,0:T(8,128)(2,1)}) custom-call(s32[4]{0:T(128)} %copy-done.14, bf16[2,224,512]{2,1,0:T(8,128)(2,1)} %copy-done.8, bf16[2,224,512]{2,1,0:T(8,128)(2,1)} %copy-done.9, ...), custom_call_target="tpu_custom_call" | custom-call | flops 11000000512 | bytes 1024 | tf_op jit(solution)/shard_map/pallas_call | solution.py:412
  68.0 4.6 %all-to-all-start = ((bf16[16,64,512]{2,1,0:T(8,128)(2,1)}), bf16[16,64,512]{2,1,0:T(8,128)(2,1)S(1)}, u32[]{:S(2)}, u32[]{:S(2)}) async-start(bf16[16,64,512]{2,1,0:T(8,128)(2,1)} %get-tuple-element.86), calls=%async_computation | async-start | bytes 2097152 | tf_op jit(solution)/shard_map/all_to_all | solution.py:463
  72.6 0.0 collective-permute-done.7.upa_ref
  72.6 0.0 copy-start.2
  72.6 0.0 collective-permute-done.8.loa_ref
  72.7 0.0 copy-start.3
  72.7 12.2 %shard_map.150 = (bf16[1,576,256]{2,1,0:T(8,128)(2,1)}, bf16[3,1,576,256]{3,2,1,0:T(8,128)(2,1)}, bf16[16,64,512]{2,1,0:T(8,128)(2,1)}) custom-call(s32[4]{0:T(128)} %copy-done.14, bf16[576,512]{1,0:T(8,128)(2,1)} %get-tuple-element.72.x_ref, bf16[576,512]{1,0:T(8,128)(2,1)} %get-tuple-element.73.g_ref, bf16[576,512]{1,0:T(8,128)(2,1)} %get-tuple-element.59.refs_0_, ...), custom_call_target="tpu_custom_call" | custom-call | flops 11000000512 | bytes 1024 | tf_op jit(solution)/shard_map/pallas_call | solution.py:412
  84.8 0.0 copy-done.2
  84.8 3.6 %all-to-all-done.a_ref = bf16[16,64,512]{2,1,0:T(8,128)(2,1)S(1)} async-done(((bf16[16,64,512]{2,1,0:T(8,128)(2,1)}), bf16[16,64,512]{2,1,0:T(8,128)(2,1)S(1)}, u32[]{:S(2)}, u32[]{:S(2)}) %all-to-all-start) | async-done | bytes 1048608 | tf_op jit(solution)/shard_map/all_to_all | solution.py:463
  88.5 4.3 %all-to-all-start.1 = ((bf16[16,64,512]{2,1,0:T(8,128)(2,1)}), bf16[16,64,512]{2,1,0:T(8,128)(2,1)S(1)}, u32[]{:S(2)}, u32[]{:S(2)}) async-start(bf16[16,64,512]{2,1,0:T(8,128)(2,1)} %get-tuple-element.87), calls=%async_computation.1 | async-start | bytes 2097152 | tf_op jit(solution)/shard_map/all_to_all | solution.py:467
  92.8 4.6 %shard_map.151 = (bf16[2,224,512]{2,1,0:T(8,128)(2,1)}, bf16[2,224,512]{2,1,0:T(8,128)(2,1)}, bf16[2,80,512]{2,1,0:T(8,128)(2,1)}, bf16[2,80,512]{2,1,0:T(8,128)(2,1)}) custom-call(bf16[1,576,256]{2,1,0:T(8,128)(2,1)} %get-tuple-element.76.a0_ref, bf16[3,1,576,256]{3,2,1,0:T(8,128)(2,1)} %get-tuple-element.77.r0_ref, ...), custom_call_target="tpu_custom_call" | custom-call | flops 4000000000 | bytes 1024 | tf_op jit(solution)/shard_map/pallas_call | solution.py:469
  97.4 3.1 %collective-permute-start.9 = (bf16[2,224,512]{2,1,0:T(8,128)(2,1)}, bf16[2,224,512]{2,1,0:T(8,128)(2,1)S(1)}, u32[]{:S(2)}, u32[]{:S(2)}) collective-permute-start(bf16[2,224,512]{2,1,0:T(8,128)(2,1)} %get-tuple-element.80), channel_id=1, source_target_pairs={{16,0},{17,1},{18,2},{19,3},{20,4},{21,5},{22,6},{23,7},{24,8},{25... | collective-permute-start | bytes 1376264 | tf_op jit(solution)/shard_map/ppermute | solution.py:316
  100.6 1.9 %collective-permute-start.10 = (bf16[2,224,512]{2,1,0:T(8,128)(2,1)}, bf16[2,224,512]{2,1,0:T(8,128)(2,1)S(1)}, u32[]{:S(2)}, u32[]{:S(2)}) collective-permute-start(bf16[2,224,512]{2,1,0:T(8,128)(2,1)} %get-tuple-element.81), channel_id=1, source_target_pairs={{224,0},{225,1},{226,2},{227,3},{228,4},{229,5},{230,6},{231,7},{2... | collective-permute-start | bytes 1376264 | tf_op jit(solution)/shard_map/ppermute | solution.py:316
  102.5 1.4 %dynamic-slice_bitcast_fusion.by_ref = bf16[128,128]{1,0:T(8,128)(2,1)} fusion(bf16[16,128,128]{2,1,0:T(8,128)(2,1)} %constant.24.clone, s32[]{:T(128)S(6)} %select_n.3), kind=kLoop, calls=%fused_computation.1 | loop fusion | bytes 65540 | tf_op jit(solution)/shard_map/squeeze | solution.py:478
  103.9 0.9 collective-permute-start.11
  104.8 0.2 collective-permute-start.12
  104.9 3.8 %all-to-all-done.1.b_ref = bf16[16,64,512]{2,1,0:T(8,128)(2,1)S(1)} async-done(((bf16[16,64,512]{2,1,0:T(8,128)(2,1)}), bf16[16,64,512]{2,1,0:T(8,128)(2,1)S(1)}, u32[]{:S(2)}, u32[]{:S(2)}) %all-to-all-start.1) | async-done | bytes 1048608 | tf_op jit(solution)/shard_map/all_to_all | solution.py:467
  108.7 1.0 copy-done.1
  109.7 2.6 %shard_map.153 = bf16[16,8,512]{2,1,0:T(8,128)(2,1)} custom-call(bf16[16,64,512]{2,1,0:T(8,128)(2,1)} %copy-done, bf16[16,64,512]{2,1,0:T(8,128)(2,1)} %copy-done.1, bf16[128,128]{1,0:T(8,128)(2,1)} %dynamic-slice_bitcast_fusion.by_ref), custom_call_target="tpu_custom_call" | custom-call | flops 2000000000 | bytes 1024 | tf_op jit(solution)/shard_map/pallas_call | solution.py:479
  112.3 7.8 %all-to-all-start.2 = ((bf16[16,8,512]{2,1,0:T(8,128)(2,1)}), bf16[16,8,512]{2,1,0:T(8,128)(2,1)S(1)}, u32[]{:S(2)}, u32[]{:S(2)}) async-start(bf16[16,8,512]{2,1,0:T(8,128)(2,1)} %shard_map.153), calls=%async_computation.2 | async-start | bytes 262144 | tf_op jit(solution)/shard_map/all_to_all | solution.py:480
  120.1 2.0 %collective-permute-done.11.eup_ref = bf16[2,80,512]{2,1,0:T(8,128)(2,1)S(1)} collective-permute-done((bf16[2,80,512]{2,1,0:T(8,128)(2,1)}, bf16[2,80,512]{2,1,0:T(8,128)(2,1)S(1)}, u32[]{:S(2)}, u32[]{:S(2)}) %collective-permute-start.11) | collective-permute-done | bytes 163872 | tf_op jit(solution)/shard_map/ppermute | solution.py:316
  122.1 0.0 collective-permute-done.12.elo_ref
  122.1 0.0 collective-permute-done.9.upb_ref
  122.1 0.0 collective-permute-done.10.lob_ref
  122.1 0.6 copy-done.12
  122.8 0.0 copy-done.13
  122.8 0.2 copy-done.6
  123.0 0.8 copy-done.7
  123.7 6.8 %shard_map.152 = (bf16[2,12,48,512]{3,2,1,0:T(8,128)(2,1)}, bf16[2,12,48,512]{3,2,1,0:T(8,128)(2,1)}) custom-call(bf16[2,12,48,512]{3,2,1,0:T(8,128)(2,1)} %x_ref.3, bf16[2,12,48,512]{3,2,1,0:T(8,128)(2,1)} %g_ref.3, bf16[2,288,512]{2,1,0:T(8,128)(2,1)} %copy-done.2, bf16[2,288,512]{2,1,0:T(8,128)(2,1)} %copy-done.3, bf16[2,224,512]{2,1,0:T(8,128)(2,1)} %copy-done.6, ...), custom_call_target="tpu_custom_call" | custom-call | flops 7000000000 | bytes 1024 | tf_op jit(solution)/shard_map/pallas_call | solution.py:474
  130.5 0.0 all-to-all-done.2
  130.6 0.6 slice_bitcast_fusion
  131.2 0.6 slice_bitcast_fusion.1
  (12 shorter events, 0.0 us)
Async XLA Ops:
  2.2 9.0 %collective-permute-start = (s32[4]{0:T(128)S(1)}, s32[4]{0:T(128)S(1)}, u32[]{:S(2)}, u32[]{:S(2)}) collective-permute-start(s32[4]{0:T(128)S(1)} %fusion), channel_id=1, source_target_pairs={{0,16},{1,17},{2,18},{3,19},{4,20},{5,21},{6,22},{7,23},{8,24},{9,... | collective-permute-start | bytes 56 | tf_op jit(solution)/shard_map/ppermute | solution.py:307
  11.2 24.6 %copy-start.14 = (s32[4]{0:T(128)}, s32[4]{0:T(128)S(1)}, u32[]{:S(2)}) copy-start(s32[4]{0:T(128)S(1)} %collective-permute-done.same_ref) | copy-start | bytes 52
  11.2 15.7 %collective-permute-start.1 = (bf16[2,288,512]{2,1,0:T(8,128)(2,1)}, bf16[2,288,512]{2,1,0:T(8,128)(2,1)S(1)}, u32[]{:S(2)}, u32[]{:S(2)}) collective-permute-start(bf16[2,288,512]{2,1,0:T(8,128)(2,1)} %get-tuple-element.49), channel_id=1, source_target_pairs={{0,16},{1,17},{2,18},{3,19},{4,20},{5,21},{6,22},{7,23},{8,24},{9,... | collective-permute-start | bytes 1769480 | tf_op jit(solution)/shard_map/ppermute | solution.py:307
  11.3 24.5 %collective-permute-start.2 = (bf16[2,288,512]{2,1,0:T(8,128)(2,1)}, bf16[2,288,512]{2,1,0:T(8,128)(2,1)S(1)}, u32[]{:S(2)}, u32[]{:S(2)}) collective-permute-start(bf16[2,288,512]{2,1,0:T(8,128)(2,1)} %get-tuple-element.50), channel_id=1, source_target_pairs={{0,224},{1,225},{2,226},{3,227},{4,228},{5,229},{6,230},{7,231},{8... | collective-permute-start | bytes 1769480 | tf_op jit(solution)/shard_map/ppermute | solution.py:307
  19.0 36.2 %collective-permute-start.3 = (bf16[2,224,512]{2,1,0:T(8,128)(2,1)}, bf16[2,224,512]{2,1,0:T(8,128)(2,1)S(1)}, u32[]{:S(2)}, u32[]{:S(2)}) collective-permute-start(bf16[2,224,512]{2,1,0:T(8,128)(2,1)} %get-tuple-element.55), channel_id=1, source_target_pairs={{0,16},{1,17},{2,18},{3,19},{4,20},{5,21},{6,22},{7,23},{8,24},{9,... | collective-permute-start | bytes 1376264 | tf_op jit(solution)/shard_map/ppermute | solution.py:307
  19.1 36.1 %collective-permute-start.4 = (bf16[2,224,512]{2,1,0:T(8,128)(2,1)}, bf16[2,224,512]{2,1,0:T(8,128)(2,1)S(1)}, u32[]{:S(2)}, u32[]{:S(2)}) collective-permute-start(bf16[2,224,512]{2,1,0:T(8,128)(2,1)} %get-tuple-element.56), channel_id=1, source_target_pairs={{0,224},{1,225},{2,226},{3,227},{4,228},{5,229},{6,230},{7,231},{8... | collective-permute-start | bytes 1376264 | tf_op jit(solution)/shard_map/ppermute | solution.py:307
  23.5 29.6 %collective-permute-start.5 = (bf16[2,80,512]{2,1,0:T(8,128)(2,1)}, bf16[2,80,512]{2,1,0:T(8,128)(2,1)S(1)}, u32[]{:S(2)}, u32[]{:S(2)}) collective-permute-start(bf16[2,80,512]{2,1,0:T(8,128)(2,1)} %get-tuple-element.57), channel_id=1, source_target_pairs={{0,31},{1,16},{2,17},{3,18},{4,19},{5,20},{6,21},{7,22},{8,23},{9,... | collective-permute-start | bytes 491528 | tf_op jit(solution)/shard_map/ppermute | solution.py:307
  26.9 8.9 %copy-start.4 = (bf16[2,288,512]{2,1,0:T(8,128)(2,1)}, bf16[2,288,512]{2,1,0:T(8,128)(2,1)S(1)}, u32[]{:S(2)}) copy-start(bf16[2,288,512]{2,1,0:T(8,128)(2,1)S(1)} %collective-permute-done.1.up_ref) | copy-start | bytes 1769476
  26.9 28.3 %collective-permute-start.6 = (bf16[2,80,512]{2,1,0:T(8,128)(2,1)}, bf16[2,80,512]{2,1,0:T(8,128)(2,1)S(1)}, u32[]{:S(2)}, u32[]{:S(2)}) collective-permute-start(bf16[2,80,512]{2,1,0:T(8,128)(2,1)} %get-tuple-element.58), channel_id=1, source_target_pairs={{0,239},{1,224},{2,225},{3,226},{4,227},{5,228},{6,229},{7,230},{8... | collective-permute-start | bytes 491528 | tf_op jit(solution)/shard_map/ppermute | solution.py:307
  35.8 0.8 copy-start.5
  53.0 19.7 %collective-permute-start.7 = (bf16[2,288,512]{2,1,0:T(8,128)(2,1)}, bf16[2,288,512]{2,1,0:T(8,128)(2,1)S(1)}, u32[]{:S(2)}, u32[]{:S(2)}) collective-permute-start(bf16[2,288,512]{2,1,0:T(8,128)(2,1)} %get-tuple-element.67), channel_id=1, source_target_pairs={{16,0},{17,1},{18,2},{19,3},{20,4},{21,5},{22,6},{23,7},{24,8},{25... | collective-permute-start | bytes 1769480 | tf_op jit(solution)/shard_map/ppermute | solution.py:316
  53.1 2.2 %copy-start.10 = (bf16[2,80,512]{2,1,0:T(8,128)(2,1)}, bf16[2,80,512]{2,1,0:T(8,128)(2,1)S(1)}, u32[]{:S(2)}) copy-start(bf16[2,80,512]{2,1,0:T(8,128)(2,1)S(1)} %collective-permute-done.5.eup_ref) | copy-start | bytes 491524
  53.1 19.6 %collective-permute-start.8 = (bf16[2,288,512]{2,1,0:T(8,128)(2,1)}, bf16[2,288,512]{2,1,0:T(8,128)(2,1)S(1)}, u32[]{:S(2)}, u32[]{:S(2)}) collective-permute-start(bf16[2,288,512]{2,1,0:T(8,128)(2,1)} %get-tuple-element.68), channel_id=1, source_target_pairs={{224,0},{225,1},{226,2},{227,3},{228,4},{229,5},{230,6},{231,7},{2... | collective-permute-start | bytes 1769480 | tf_op jit(solution)/shard_map/ppermute | solution.py:316
  55.2 0.7 copy-start.11
  55.2 0.8 copy-start.8
  55.3 0.9 copy-start.9
  68.0 20.5 %all-to-all-start = ((bf16[16,64,512]{2,1,0:T(8,128)(2,1)}), bf16[16,64,512]{2,1,0:T(8,128)(2,1)S(1)}, u32[]{:S(2)}, u32[]{:S(2)}) async-start(bf16[16,64,512]{2,1,0:T(8,128)(2,1)} %get-tuple-element.86), calls=%async_computation | async-start | bytes 2097152 | tf_op jit(solution)/shard_map/all_to_all | solution.py:463
  72.6 12.2 %copy-start.2 = (bf16[2,288,512]{2,1,0:T(8,128)(2,1)}, bf16[2,288,512]{2,1,0:T(8,128)(2,1)S(1)}, u32[]{:S(2)}) copy-start(bf16[2,288,512]{2,1,0:T(8,128)(2,1)S(1)} %collective-permute-done.7.upa_ref) | copy-start | bytes 1769476
  72.7 12.2 %copy-start.3 = (bf16[2,288,512]{2,1,0:T(8,128)(2,1)}, bf16[2,288,512]{2,1,0:T(8,128)(2,1)S(1)}, u32[]{:S(2)}) copy-start(bf16[2,288,512]{2,1,0:T(8,128)(2,1)S(1)} %collective-permute-done.8.loa_ref) | copy-start | bytes 1769476
  88.5 9.0 %copy-start = (bf16[16,64,512]{2,1,0:T(8,128)(2,1)}, bf16[16,64,512]{2,1,0:T(8,128)(2,1)S(1)}, u32[]{:S(2)}) copy-start(bf16[16,64,512]{2,1,0:T(8,128)(2,1)S(1)} %all-to-all-done.a_ref) | copy-start | bytes 3145732
  88.5 20.2 %all-to-all-start.1 = ((bf16[16,64,512]{2,1,0:T(8,128)(2,1)}), bf16[16,64,512]{2,1,0:T(8,128)(2,1)S(1)}, u32[]{:S(2)}, u32[]{:S(2)}) async-start(bf16[16,64,512]{2,1,0:T(8,128)(2,1)} %get-tuple-element.87), calls=%async_computation.1 | async-start | bytes 2097152 | tf_op jit(solution)/shard_map/all_to_all | solution.py:467
  97.4 24.7 %collective-permute-start.9 = (bf16[2,224,512]{2,1,0:T(8,128)(2,1)}, bf16[2,224,512]{2,1,0:T(8,128)(2,1)S(1)}, u32[]{:S(2)}, u32[]{:S(2)}) collective-permute-start(bf16[2,224,512]{2,1,0:T(8,128)(2,1)} %get-tuple-element.80), channel_id=1, source_target_pairs={{16,0},{17,1},{18,2},{19,3},{20,4},{21,5},{22,6},{23,7},{24,8},{25... | collective-permute-start | bytes 1376264 | tf_op jit(solution)/shard_map/ppermute | solution.py:316
  100.6 21.5 %collective-permute-start.10 = (bf16[2,224,512]{2,1,0:T(8,128)(2,1)}, bf16[2,224,512]{2,1,0:T(8,128)(2,1)S(1)}, u32[]{:S(2)}, u32[]{:S(2)}) collective-permute-start(bf16[2,224,512]{2,1,0:T(8,128)(2,1)} %get-tuple-element.81), channel_id=1, source_target_pairs={{224,0},{225,1},{226,2},{227,3},{228,4},{229,5},{230,6},{231,7},{2... | collective-permute-start | bytes 1376264 | tf_op jit(solution)/shard_map/ppermute | solution.py:316
  103.9 18.2 %collective-permute-start.11 = (bf16[2,80,512]{2,1,0:T(8,128)(2,1)}, bf16[2,80,512]{2,1,0:T(8,128)(2,1)S(1)}, u32[]{:S(2)}, u32[]{:S(2)}) collective-permute-start(bf16[2,80,512]{2,1,0:T(8,128)(2,1)} %get-tuple-element.82), channel_id=1, source_target_pairs={{31,0},{16,1},{17,2},{18,3},{19,4},{20,5},{21,6},{22,7},{23,8},{24... | collective-permute-start | bytes 491528 | tf_op jit(solution)/shard_map/ppermute | solution.py:316
  104.8 17.3 %collective-permute-start.12 = (bf16[2,80,512]{2,1,0:T(8,128)(2,1)}, bf16[2,80,512]{2,1,0:T(8,128)(2,1)S(1)}, u32[]{:S(2)}, u32[]{:S(2)}) collective-permute-start(bf16[2,80,512]{2,1,0:T(8,128)(2,1)} %get-tuple-element.83), channel_id=1, source_target_pairs={{239,0},{224,1},{225,2},{226,3},{227,4},{228,5},{229,6},{230,7},{2... | collective-permute-start | bytes 491528 | tf_op jit(solution)/shard_map/ppermute | solution.py:316
  108.7 1.0 copy-start.1
  112.3 18.2 %all-to-all-start.2 = ((bf16[16,8,512]{2,1,0:T(8,128)(2,1)}), bf16[16,8,512]{2,1,0:T(8,128)(2,1)S(1)}, u32[]{:S(2)}, u32[]{:S(2)}) async-start(bf16[16,8,512]{2,1,0:T(8,128)(2,1)} %shard_map.153), calls=%async_computation.2 | async-start | bytes 262144 | tf_op jit(solution)/shard_map/all_to_all | solution.py:480
  122.1 0.7 copy-start.12
  122.1 0.7 copy-start.13
  122.1 0.9 copy-start.6
  123.0 0.8 copy-start.7
where the time goes:
time: 133 us; the launch traced here: 132 us
  Pallas kernels  59.7 us (45%)
  starting transfers between devices  51.8 us (39%)
  waiting for transfers between devices  10.9 us (8%)
  local copies, waits for them, and re-layouts  8.46 us (6%)
    ppermute x7, starting transfers between devices, send(): return lax.ppermute(x, ('lat', 'lon'), pairs)  26.7 us
    pallas_call x2, Pallas kernels, second_chunk(): call(kernel, 11, grid=(1,), in_specs=[pl.BlockSpec(memory_space=pltpu.SME...  24 us
    pallas_call x1, Pallas kernels, first_chunk(): call(chunk_a_kernel, 15, grid=(GROUPS,), in_specs=[pl.BlockSpec(memory_sp...  16.3 us
    ppermute x6, starting transfers between devices, unsend(): return lax.ppermute(x, ('lat', 'lon'), pairs)  8.3 us
    all_to_all x1, starting transfers between devices, shards(): part = lax.all_to_all(part, 'lat', 0, 0).astype(f32).sum(0)  7.83 us
    pallas_call x1, Pallas kernels, shards(): call(behind_kernel, 7, out_shape=[shaped(*features.shape)] * 2)  6.78 us
    pallas_call x1, Pallas kernels, shards(): call(ahead_kernel, 4, out_shape=[shaped(*s) for s in (a, a, b, b, edge, e...  5.39 us
    pallas_call x1, Pallas kernels, shards(): call(back_b_kernel, 4, out_shape=[shaped(*s) for s in (b, b, edge, edge)])  4.65 us
  transfers between devices with their start and end apart: 16, of which 4 were waited for; matrix products, arithmetic and copies ran while one was open for 1% of the time, Pallas kernels for 45%

commit v1 on v0

v1 whole, which is shorter than its diff:
```python
import functools

import jax
import jax.numpy as jnp
import numpy as np
from jax import lax
from jax.experimental import pallas as pl
from jax.experimental.pallas import tpu as pltpu
from jax.sharding import PartitionSpec as P

HEADS = 8
WINDOW = 12
SHIFT = 6
LEV, ROWS, COLS, D = 2, 12, 48, 512
LATS, LONS = 16, 16
HALF = LEV * SHIFT * COLS
WINS = COLS // WINDOW
TOK = HALF // WINS
WTOK = 2 * TOK
RIM = LEV * SHIFT * SHIFT
RIMP = 80
PACKED = HALF - RIM + 8
QUAD = 256
GROUPS = D // QUAD
HPG = 4
HD = 64
CHUNK = 2
CTOK = CHUNK * WTOK
SPLIT = CHUNK * TOK
LOG2E = 1.4426950408889634
VMEM = 60 * 1024 * 1024
NT = (((1,), (1,)), ((), ()))
TN = (((0,), (0,)), ((), ()))
f32, bf16 = jnp.float32, jnp.bfloat16
SPAN = 3 * D // (LATS * LONS)
SPAN_OUT = D // (LATS * LONS)
GW = 3 * QUAD // LONS
GO = SPAN_OUT * LATS
READY = GROUPS * GW + GO
FLAGS = 16


EARLY = 32


def one_hots():
    early = np.zeros((SPLIT, LEV * SHIFT * EARLY), np.float32)
    late = np.zeros((PACKED - SPLIT, HALF), np.float32)
    place = np.zeros((PACKED, HALF), np.float32)
    cut = np.zeros((RIMP, HALF), np.float32)
    for line in range(LEV * SHIFT):
        for col in range(COLS - SHIFT):
            win, at = divmod(col, WINDOW)
            wide = WINDOW if win < WINS - 1 else SHIFT
            to = win * TOK + line * wide + at
            place[to, line * COLS + col + SHIFT] = 1
            if win < CHUNK:
                early[to, line * EARLY + col + SHIFT] = 1
            else:
                late[to - SPLIT, line * COLS + col + SHIFT] = 1
        for col in range(SHIFT):
            cut[line * SHIFT + col, line * COLS + col] = 1
    return early, late, place, cut


def orders():
    by_lon = np.zeros((2, GROUPS, LONS * GW, 3 * QUAD), np.float32)
    out_by_lon = np.zeros((2, D, D), np.float32)
    by_lat = np.zeros((LONS, LATS * 8, LATS * 8), np.float32)

    def place(core, lon):
        return (lon % 2 ^ core) * LONS // 2 + lon // 2

    for group in range(GROUPS):
        filled = [0] * LONS
        for row in range(3 * QUAD):
            column = row // QUAD * D + group * QUAD + row % QUAD
            device, at = divmod(column, SPAN)
            lat, lon = divmod(device, LONS)
            for core in range(2):
                by_lon[core, group, place(core, lon) * GW + filled[lon], row] = 1
            by_lat[lon, lat * 8 + at, group * GW + filled[lon]] = 1
            filled[lon] += 1
        assert filled == [GW] * LONS
    for row in range(D):
        device, at = divmod(row, SPAN_OUT)
        lat, lon = divmod(device, LONS)
        for core in range(2):
            out_by_lon[core, place(core, lon) * GO + lat * SPAN_OUT + at, row] = 1
    for lat in range(LATS):
        for at in range(SPAN_OUT):
            by_lat[:, lat * 8 + SPAN + at, GROUPS * GW + lat * SPAN_OUT + at] = 1
    return by_lon, out_by_lon, by_lat


EARLY_PLACE, LATE_PLACE, PLACE, CUT = one_hots()
BY_LON, OUT_BY_LON, BY_LAT = orders()


def mm(a, b, dims=(((1,), (0,)), ((), ()))):
    return lax.dot_general(a, b, dims, preferred_element_type=f32)


def move(one_hot, x):
    return mm(one_hot, x).astype(bf16)


def normalize(x):
    c = x - jnp.mean(x, axis=-1, keepdims=True)
    return c * lax.rsqrt(jnp.mean(c * c, axis=-1, keepdims=True) + 1e-5)


def early_kernel(x_ref, g_ref, regions_ref, place_ref, up_ref, lo_ref, n_s):
    for lev in range(LEV):
        x = x_ref[lev].reshape(ROWS * EARLY, D).astype(f32)
        n_s[lev] = normalize(x).astype(bf16).reshape(ROWS, EARLY, D)
    for at, src in enumerate((n_s, g_ref)):
        lower = src[:, :SHIFT].reshape(LEV * SHIFT * EARLY, D)
        upper = src[:, SHIFT:].reshape(LEV * SHIFT * EARLY, D)
        up_ref[at, :SPLIT] = move(place_ref[...], upper)
        lo_ref[at] = move(place_ref[...], lower)
        up_ref[at, SPLIT:] = jnp.zeros((FLAGS, D), bf16)
    same = jnp.where(regions_ref[0:1] == regions_ref[SHIFT : SHIFT + 1], 1.0, 0.0)
    row = lax.broadcasted_iota(jnp.int32, (COLS, D), 0)
    lane = lax.broadcasted_iota(jnp.int32, (COLS, D), 1)
    spread = jnp.where(row == lane, 1.0, 0.0).astype(bf16)
    up_ref[0, SPLIT:] = move(jnp.broadcast_to(same, (FLAGS, COLS)).astype(bf16), spread)


def late_kernel(x_ref, g_ref, place_ref, cut_ref, up_ref, lo_ref, eup_ref, elo_ref, n_s):
    for lev in range(LEV):
        x = x_ref[lev].reshape(ROWS * COLS, D).astype(f32)
        n_s[lev] = normalize(x).astype(bf16).reshape(ROWS, COLS, D)
    for at, src in enumerate((n_s, g_ref)):
        for rows, dst, rim in (
            (slice(SHIFT, ROWS), up_ref, eup_ref),
            (slice(0, SHIFT), lo_ref, elo_ref),
        ):
            half = src[:, rows].reshape(HALF, D)
            dst[at] = move(place_ref[...], half)
            rim[at] = move(cut_ref[...], half)


def attend(flags, first, group, x_s, g_s, wqkv_s, wout_s, att_s, rows_s, scratch):
    k_s, v_s, s_s, dp_s, p_s, ds_s, qs_s, gs_s = scratch
    lane = lax.broadcasted_iota(jnp.int32, (1, QUAD), 1)
    head_of = lane // HD
    at = group * QUAD
    wq, wk, wv = (wqkv_s[:, D * i + at : D * i + at + QUAD] for i in range(3))
    wo = wout_s[at : at + QUAD]
    query = lax.broadcasted_iota(jnp.int32, (1, HPG * WTOK), 1)
    in_upper = lax.rem(query, WTOK) < TOK

    def project(w):
        rows = slice(w * WTOK, (w + 1) * WTOK)
        x = x_s[rows]
        k_s[rows] = mm(x, wk).astype(bf16)
        v_s[rows] = mm(x, wv).astype(bf16)
        q = mm(x, wq).astype(bf16)
        a = mm(g_s[rows], wo, NT).astype(bf16)
        for h in range(HPG):
            qs_s[w, h * WTOK : (h + 1) * WTOK] = jnp.where(head_of == h, q, jnp.zeros_like(q))
            gs_s[w, h * WTOK : (h + 1) * WTOK] = jnp.where(head_of == h, a, jnp.zeros_like(a))

    def score(w, cols):
        rows = slice(w * WTOK, (w + 1) * WTOK)
        s_s[w, :, cols] = mm(k_s[rows], qs_s[w, cols], NT)
        dp_s[w, :, cols] = mm(v_s[rows], gs_s[w, cols], NT)

    def soften(w, cols):
        here = lax.broadcasted_iota(jnp.int32, (1, D), 1) == WINDOW * (first + w)
        flag = jnp.sum(jnp.where(here, flags, 0.0), axis=1, keepdims=True)
        same = jnp.broadcast_to(flag, (1, 128)) > 0.5
        up = in_upper[:, cols]
        s_up, s_lo = s_s[w, :TOK, cols], s_s[w, TOK:, cols]
        m_up = jnp.max(s_up, axis=0, keepdims=True)
        m_lo = jnp.max(s_lo, axis=0, keepdims=True)
        m = jnp.where(same, jnp.maximum(m_up, m_lo), jnp.where(up, m_up, m_lo))
        from_up = jnp.where(jnp.logical_or(same, up), m, 1e30)
        from_lo = jnp.where(jnp.logical_and(jnp.logical_not(same), up), 1e30, m)
        c = LOG2E * HD**-0.5
        e_up = jnp.exp2((s_up - from_up) * c)
        e_lo = jnp.exp2((s_lo - from_lo) * c)
        total = jnp.sum(e_up, axis=0, keepdims=True) + jnp.sum(e_lo, axis=0, keepdims=True)
        p = jnp.concatenate([e_up, e_lo], axis=0) * (1.0 / total)
        p_s[w, :, cols] = p.astype(bf16)
        dp = dp_s[w, :, cols]
        delta = jnp.sum(dp * p, axis=0, keepdims=True)
        ds_s[w, :, cols] = (p * ((dp - delta) * HD**-0.5)).astype(bf16)

    def pick(stack):
        out = stack[:WTOK]
        for h in range(1, HPG):
            out = jnp.where(head_of == h, stack[h * WTOK : (h + 1) * WTOK], out)
        return out.astype(bf16)

    def finish(w, part):
        rows = slice(w * WTOK, (w + 1) * WTOK)
        if part == 0:
            att_s[group, rows] = pick(mm(p_s[w], v_s[rows], TN))
        elif part == 1:
            rows_s[group, 0, rows] = pick(mm(ds_s[w], k_s[rows], TN))
        elif part == 2:
            rows_s[group, 1, rows] = mm(ds_s[w], qs_s[w]).astype(bf16)
        else:
            rows_s[group, 2, rows] = mm(p_s[w], gs_s[w]).astype(bf16)

    wide = HPG * WTOK
    tiles = [slice(i, min(i + 256, wide)) for i in range(0, wide, 256)]
    for t in range(CHUNK):
        project(t)
        for tile in tiles:
            score(t, tile)
            for i in range(tile.start, tile.stop, 128):
                soften(t, slice(i, i + 128))
        for j in range(4):
            finish(t, j)


def starts(pairs, sems):
    copies = [pltpu.make_async_copy(src, dst, sems.at[i]) for i, (src, dst) in enumerate(pairs)]
    for copy in copies:
        copy.start()
    return copies


def waits(copies):
    for copy in copies:
        copy.wait()


def whole_windows(up, lo, at, dst, count):
    pairs = []
    for w in range(count):
        for half, src in enumerate((up, lo)):
            to = w * WTOK + half * TOK
            pairs.append((src.at[at, pl.ds(w * TOK, TOK)], dst.at[pl.ds(to, TOK)]))
    return pairs


def chunk_a_kernel(up, lo, wqkv, wout, att, rows, rup, rlo, *refs):
    x_s, g_s, flag_s, wqkv_s, wout_s, att_s, rows_s, rup_s, rlo_s, in_sems, out_sems = refs[:11]
    scratch = refs[11:]
    copies = starts(
        [
            *whole_windows(up, lo, 0, x_s, CHUNK),
            (wqkv, wqkv_s),
            (up.at[0, pl.ds(SPLIT, FLAGS)], flag_s),
            *whole_windows(up, lo, 1, g_s, CHUNK),
            (wout, wout_s),
        ],
        in_sems,
    )
    waits(copies)
    flags = flag_s[...].astype(f32)[0:1]
    outs = []
    for group in range(GROUPS):
        attend(flags, 0, group, x_s, g_s, wqkv_s, wout_s, att_s, rows_s, scratch)
        pairs = [(att_s.at[group], att.at[group]), (rows_s.at[group], rows.at[group])]
        outs += starts(pairs, out_sems.at[pl.ds(2 * group, 2)])
    back(False, att_s, rows_s, wqkv_s, wout_s, rup_s, rlo_s)
    outs += starts([(rup_s, rup), (rlo_s, rlo)], out_sems.at[pl.ds(2 * GROUPS, 2)])
    waits(outs)


def chunk_b_kernel(
    core_ref, upa, loa, up, lo, eup, elo, wqkv, wout, atta, rowsa, by_lon, out_by_lon,
    att, rows, mine, theirs, *refs,
):
    x_s, g_s, flag_s, wqkv_s, wout_s, att_s, rows_s, in_sems, out_sems, late_sems = refs[:10]
    here_s, there_s, xa_s, ga_s, atta_s, rowsa_s, by_s, out_by_s, o_s = refs[10:19]
    scratch = refs[19:]
    core = core_ref[0]
    last = pl.ds((CHUNK - 1) * TOK, RIMP)
    copies = starts(
        [
            *whole_windows(up, lo, 0, x_s, CHUNK - 1),
            *whole_windows(up, lo, 1, g_s, CHUNK - 1),
            (up.at[:, last], here_s.at[0]),
            (lo.at[:, last], here_s.at[1]),
            (eup, there_s.at[0]),
            (elo, there_s.at[1]),
            (wqkv, wqkv_s),
            (wout, wout_s),
            (upa.at[0, pl.ds(SPLIT, FLAGS)], flag_s),
        ],
        in_sems,
    )
    late = starts(
        [
            *whole_windows(upa, loa, 0, xa_s, CHUNK),
            *whole_windows(upa, loa, 1, ga_s, CHUNK),
            (atta, atta_s),
            (rowsa, rowsa_s),
            (by_lon.at[core], by_s),
            (out_by_lon.at[core], out_by_s),
        ],
        late_sems,
    )
    waits(copies)
    for at, dst in enumerate((x_s, g_s)):
        for half in range(2):
            here = here_s[half, at].astype(f32)[:RIM]
            there = there_s[half, at].astype(f32)[:RIM]
            to = (CHUNK - 1) * WTOK + half * TOK
            dst[to : to + TOK] = jnp.concatenate([here, there], axis=0).astype(bf16)
    flags = flag_s[...].astype(f32)[0:1]
    outs = []
    for group in range(GROUPS):
        attend(flags, CHUNK, group, x_s, g_s, wqkv_s, wout_s, att_s, rows_s, scratch)
        pairs = [(att_s.at[group], att.at[group]), (rows_s.at[group], rows.at[group])]
        outs += starts(pairs, out_sems.at[pl.ds(2 * group, 2)])
        if group == 0:
            waits(late)
        parts = []
        for i in range(3):
            total = mm(rowsa_s[group, i], xa_s[...], TN) + mm(rows_s[group, i], x_s[...], TN)
            parts.append(total.astype(bf16))
        ready = move(by_s[group], jnp.concatenate(parts, axis=0))
        o_s[:, :, group * GW : (group + 1) * GW] = ready.reshape(2, LONS // 2, GW, D)
        out = (mm(ga_s[...], atta_s[group], TN) + mm(g_s[...], att_s[group], TN)).astype(bf16)
        out = move(out_by_s[...], out).reshape(2, LONS // 2, GO, QUAD)
        o_s[:, :, GROUPS * GW :, group * QUAD : (group + 1) * QUAD] = out
    outs += starts([(o_s.at[0], mine), (o_s.at[1], theirs)], out_sems.at[pl.ds(2 * GROUPS, 2)])
    waits(outs)


def back(rimmed, att_s, rows_s, wqkv_s, wout_s, up_ref, lo_ref, *edges):
    for w in range(CHUNK):
        rows = slice(w * WTOK, (w + 1) * WTOK)
        branch = gn = 0.0
        for i in range(GROUPS):
            branch = branch + mm(att_s[i, rows], wout_s[QUAD * i : QUAD * (i + 1)])
            for j in range(3):
                at = D * j + QUAD * i
                gn = gn + mm(rows_s[i, j, rows], wqkv_s[:, at : at + QUAD], NT)
        for at, full in enumerate((branch, gn)):
            for half, dst in enumerate((up_ref, lo_ref)):
                part = full[half * TOK : (half + 1) * TOK]
                if rimmed and w == CHUNK - 1:
                    pad = jnp.zeros((8, D), f32)
                    dst[at, w * TOK :] = jnp.concatenate([part[:RIM], pad], axis=0).astype(bf16)
                    edges[half][at] = jnp.concatenate([part[RIM:], pad], axis=0).astype(bf16)
                else:
                    dst[at, w * TOK : (w + 1) * TOK] = part.astype(bf16)


def back_b_kernel(att_ref, rows_ref, wqkv_ref, wout_ref, *outs):
    back(True, att_ref, rows_ref, wqkv_ref, wout_ref, *outs)


def behind_kernel(
    x_ref, g_ref, upa_ref, loa_ref, upb_ref, lob_ref, eup_ref, elo_ref, place_ref, cut_ref,
    o_ref, gf_ref,
):
    def finish(a_ref, b_ref, e_ref):
        both = []
        for at in range(2):
            both.append(
                mm(place_ref[:, :SPLIT], a_ref[at])
                + mm(place_ref[:, SPLIT:], b_ref[at])
                + mm(cut_ref[...], e_ref[at])
            )
        branch, gn = both
        x = x_ref[...].reshape(HALF, D).astype(f32)
        c = x - jnp.mean(x, axis=-1, keepdims=True)
        rstd = lax.rsqrt(jnp.mean(c * c, axis=-1, keepdims=True) + 1e-5)
        xhat = c * rstd
        o_ref[...] = (x + branch).astype(bf16).reshape(LEV, SHIFT, COLS, D)
        along = jnp.mean(gn * xhat, axis=-1, keepdims=True)
        dx = rstd * (gn - jnp.mean(gn, axis=-1, keepdims=True) - xhat * along)
        g = g_ref[...].reshape(HALF, D).astype(f32)
        gf_ref[...] = (g + dx).astype(bf16).reshape(LEV, SHIFT, COLS, D)

    @pl.when(pl.program_id(0) == 0)
    def _():
        finish(loa_ref, lob_ref, elo_ref)

    @pl.when(pl.program_id(0) == 1)
    def _():
        finish(upa_ref, upb_ref, eup_ref)


def sum_kernel(parts_ref, by_ref, o_ref):
    total = parts_ref[0].astype(f32)
    for i in range(1, LONS // 2):
        total = total + parts_ref[i].astype(f32)
    o_ref[...] = move(by_ref[...], total.astype(bf16)).reshape(LATS, 8, D)


def send(x, place):
    pairs = []
    for i in range(LATS):
        for j in range(LONS):
            lat, lon = place(i, j)
            pairs.append((i * LONS + j, lat % LATS * LONS + lon % LONS))
    return lax.ppermute(x, ("lat", "lon"), pairs)


def unsend(x, place):
    pairs = []
    for i in range(LATS):
        for j in range(LONS):
            lat, lon = place(i, j)
            pairs.append((lat % LATS * LONS + lon % LONS, i * LONS + j))
    return lax.ppermute(x, ("lat", "lon"), pairs)


def to_upper(i, j):
    return i ^ 1, j


def to_lower(i, j):
    return (i, j) if i % 2 else (i - 2, j)


def to_upper_rim(i, j):
    return i ^ 1, j - 1


def to_lower_rim(i, j):
    return (i, j - 1) if i % 2 else (i - 2, j - 1)


def shaped(*shape, dtype=bf16):
    return jax.ShapeDtypeStruct(shape, dtype)


def call(kernel, us, **kwargs):
    cost = pl.CostEstimate(flops=int(us * 1e9), bytes_accessed=1024, transcendentals=0)
    params = pltpu.CompilerParams(vmem_limit_bytes=VMEM)
    return pl.pallas_call(kernel, cost_estimate=cost, compiler_params=params, **kwargs)


def whole(shape):
    return pl.BlockSpec(shape, lambda *_: (0,) * len(shape))


def fixed(shape):
    return pl.BlockSpec(shape, lambda *_: (0,) * len(shape), pipeline_mode=pl.Buffered(1))


def anywhere(count):
    return [pl.BlockSpec(memory_space=pl.ANY)] * count


def scratches():
    stack = HPG * WTOK
    return [
        *[pltpu.VMEM((CTOK, QUAD), bf16)] * 2,
        *[pltpu.VMEM((CHUNK, WTOK, stack), f32)] * 2,
        *[pltpu.VMEM((CHUNK, WTOK, stack), bf16)] * 2,
        *[pltpu.VMEM((CHUNK, stack, QUAD), bf16)] * 2,
    ]


def common():
    return [
        pltpu.VMEM((CTOK, D), bf16),
        pltpu.VMEM((CTOK, D), bf16),
        pltpu.VMEM((FLAGS, D), bf16),
        pltpu.VMEM((D, 3 * D), bf16),
        pltpu.VMEM((D, D), bf16),
        pltpu.VMEM((GROUPS, CTOK, QUAD), bf16),
        pltpu.VMEM((GROUPS, 3, CTOK, QUAD), bf16),
    ]


ATT, ROWSET = (GROUPS, CTOK, QUAD), (GROUPS, 3, CTOK, QUAD)


def first_chunk(up, lo, qkv_weight, out_weight):
    ret = (2, SPLIT, D)
    return call(
        chunk_a_kernel,
        13,
        in_specs=anywhere(4),
        out_specs=anywhere(4),
        out_shape=[shaped(*o) for o in (ATT, ROWSET, ret, ret)],
        scratch_shapes=[
            *common(),
            pltpu.VMEM(ret, bf16),
            pltpu.VMEM(ret, bf16),
            pltpu.SemaphoreType.DMA((4 * CHUNK + 3,)),
            pltpu.SemaphoreType.DMA((2 * GROUPS + 2,)),
            *scratches(),
        ],
    )(up, lo, qkv_weight, out_weight)


def second_chunk(core, upa, loa, up, lo, eup, elo, qkv_weight, out_weight, att, rows):
    by_lon, out_by_lon = jnp.asarray(BY_LON, bf16), jnp.asarray(OUT_BY_LON, bf16)
    ready = (LONS // 2, READY, D)
    return call(
        chunk_b_kernel,
        18,
        in_specs=[pl.BlockSpec(memory_space=pltpu.SMEM)] + anywhere(12),
        out_specs=anywhere(4),
        out_shape=[shaped(*o) for o in (ATT, ROWSET, ready, ready)],
        scratch_shapes=[
            *common(),
            pltpu.SemaphoreType.DMA((4 * (CHUNK - 1) + 7,)),
            pltpu.SemaphoreType.DMA((2 * GROUPS + 2,)),
            pltpu.SemaphoreType.DMA((4 * CHUNK + 4,)),
            pltpu.VMEM((2, 2, RIMP, D), bf16),
            pltpu.VMEM((2, 2, RIMP, D), bf16),
            pltpu.VMEM((CTOK, D), bf16),
            pltpu.VMEM((CTOK, D), bf16),
            pltpu.VMEM(ATT, bf16),
            pltpu.VMEM(ROWSET, bf16),
            pltpu.VMEM(by_lon.shape[1:], bf16),
            pltpu.VMEM(out_by_lon.shape[1:], bf16),
            pltpu.VMEM((2, *ready), bf16),
            *scratches(),
        ],
    )(core, upa, loa, up, lo, eup, elo, qkv_weight, out_weight, att, rows, by_lon, out_by_lon)


def other_core(i, j):
    return i, j ^ 1


def shards(features, regions, qkv_weight, out_weight, grad_output):
    place, cut = jnp.asarray(PLACE, bf16), jnp.asarray(CUT, bf16)
    core = (lax.axis_index("lon") % 2).reshape(1)
    a, b, edge = (2, SPLIT, D), (2, PACKED - SPLIT, D), (2, RIMP, D)
    early = pl.BlockSpec((LEV, ROWS, EARLY, D), lambda i: (0, 0, 0, 0))
    up_shape = (2, SPLIT + FLAGS, D)
    upa, loa = call(
        early_kernel,
        3,
        grid=(1,),
        in_specs=[early, early, whole(regions.shape), whole(EARLY_PLACE.shape)],
        out_specs=[whole(up_shape), whole(a)],
        out_shape=[shaped(*up_shape), shaped(*a)],
        scratch_shapes=[pltpu.VMEM((LEV, ROWS, EARLY, D), bf16)],
    )(features, grad_output, regions, jnp.asarray(EARLY_PLACE, bf16))
    features, grad_output, upa, loa = lax.optimization_barrier((features, grad_output, upa, loa))
    upa, loa = send(upa, to_upper), send(loa, to_lower)
    upb, lob, eup, elo = call(
        late_kernel,
        5,
        out_shape=[shaped(*s) for s in (b, b, edge, edge)],
        scratch_shapes=[pltpu.VMEM((LEV, ROWS, COLS, D), bf16)],
    )(features, grad_output, jnp.asarray(LATE_PLACE, bf16), cut)
    upb, lob = send(upb, to_upper), send(lob, to_lower)
    eup, elo = send(eup, to_upper_rim), send(elo, to_lower_rim)
    weights = (qkv_weight, out_weight)

    atta, rowsa, rupa, rloa = first_chunk(upa, loa, *weights)
    atta, rupa, rloa = lax.optimization_barrier((atta, rupa, rloa))
    rupa, rloa = unsend(rupa, to_upper), unsend(rloa, to_lower)
    attb, rowsb, mine, theirs = second_chunk(
        core, upa, loa, upb, lob, eup, elo, *weights, atta, rowsa
    )
    attb, mine, theirs, rupa, rloa = lax.optimization_barrier((attb, mine, theirs, rupa, rloa))
    theirs = send(theirs, other_core)

    rupb, rlob, reup, relo = call(
        back_b_kernel, 4, out_shape=[shaped(*s) for s in (b, b, edge, edge)]
    )(attb, rowsb, *weights)
    ready = (mine.astype(f32) + theirs.astype(f32)).astype(bf16)
    ready, rupb, rlob, reup, relo = lax.optimization_barrier((ready, rupb, rlob, reup, relo))
    cores = [list(range(i, LONS, 2)) for i in range(2)]
    parts = lax.all_to_all(ready, "lon", 0, 0, axis_index_groups=cores)
    rupb, rlob = unsend(rupb, to_upper), unsend(rlob, to_lower)
    reup, relo = unsend(reup, to_upper_rim), unsend(relo, to_lower_rim)
    half = pl.BlockSpec((LEV, SHIFT, COLS, D), lambda i: (0, i, 0, 0))
    returned = (rupa, rloa, rupb, rlob, reup, relo, place.T, cut.T)
    output, grad_features = call(
        behind_kernel,
        6,
        grid=(2,),
        in_specs=[half, half] + [fixed(r.shape) for r in returned],
        out_specs=[half, half],
        out_shape=[shaped(*features.shape)] * 2,
    )(features, grad_output, *returned)

    by_lat = jnp.asarray(BY_LAT, bf16)[lax.axis_index("lon")]
    part = call(sum_kernel, 2, out_shape=shaped(LATS, 8, D))(parts, by_lat)
    part = lax.all_to_all(part, "lat", 0, 0).astype(f32).sum(0)
    return (output, grad_features, part[:SPAN].T, part[SPAN:].T)


def solution(mesh):
    return jax.shard_map(
        shards,
        mesh=mesh,
        in_specs=(
            P(None, "lat", "lon", None),
            P("lat", "lon"),
            P(),
            P(),
            P(None, "lat", "lon", None),
        ),
        out_specs=(
            P(None, "lat", "lon", None),
            P(None, "lat", "lon", None),
            P(None, ("lat", "lon")),
            P(None, ("lat", "lon")),
        ),
        check_vma=False,
    )
```

time: 133 us -> 123 us (0.925)
  starting transfers between devices: 51.8 us -> 43.5 us
  Pallas kernels: 59.7 us -> 56.5 us
  waiting for transfers between devices: 10.9 us -> 12.8 us
  local copies, waits for them, and re-layouts: 8.46 us -> 6.87 us
    all_to_all x2 -> x1, starting transfers between devices: 8.96 us -> 4.35 us  [shards(): parts = lax.all_to_all(ready, 'lon', 0, 0, axis_index_groups=cores)]
    pallas_call x6, Pallas kernels: 55.1 us -> 51.5 us  [the longest x1 20.9 us: second_chunk(): call(chunk_b_kernel, 18, in_specs=[pl.BlockSpec(memory_space=pltpu.SMEM)]...]
    all_to_all x1, starting transfers between devices: 7.83 us -> 4.84 us  [shards(): part = lax.all_to_all(part, 'lat', 0, 0).astype(f32).sum(0)]
    ppermute x6, waiting for transfers between devices: 1.98 us -> 4.69 us  [unsend(): return lax.ppermute(x, ('lat', 'lon'), pairs)]
    slice x2 -> x0, local copies, waits for them, and re-layouts: 1.54 us -> none  [shards(): same = (regions[0, ::WINDOW] == regions[SHIFT, ::WINDOW]).astype(jnp.int32)]
    ppermute x7, waiting for transfers between devices: 1.5 us -> 0.02 us  [send(): return lax.ppermute(x, ('lat', 'lon'), pairs)]
    ppermute x7, starting transfers between devices: 26.7 us -> 25.2 us  [send(): return lax.ppermute(x, ('lat', 'lon'), pairs)]
    all_to_all x2 -> x1, waiting for transfers between devices: 7.4 us -> 8.11 us  [shards(): parts = lax.all_to_all(ready, 'lon', 0, 0, axis_index_groups=cores)]
  transfers between devices with their start and end apart: 16 -> 15, of which waited for: 4 -> 2; matrix products, arithmetic and copies ran while one was open for 1% -> 1% of each run, Pallas kernels for 45% -> 43%
where the time goes in v1:
time: 123 us; the launch traced here: 122 us
  Pallas kernels  56.5 us (46%)
  starting transfers between devices  43.5 us (35%)
  waiting for transfers between devices  12.8 us (10%)
  local copies, waits for them, and re-layouts  6.87 us (6%)
  other arithmetic  1.31 us (1%)
    ppermute x7, starting transfers between devices, send(): return lax.ppermute(x, ('lat', 'lon'), pairs)  25.2 us
    pallas_call x1, Pallas kernels, second_chunk(): call(chunk_b_kernel, 18, in_specs=[pl.BlockSpec(memory_space=pltpu.SMEM)]...  20.9 us
    pallas_call x1, Pallas kernels, first_chunk(): call(chunk_a_kernel, 13, in_specs=anywhere(4), out_specs=anywhere(4), out...  13.7 us
    ppermute x6, starting transfers between devices, unsend(): return lax.ppermute(x, ('lat', 'lon'), pairs)  9.07 us
    all_to_all x1, waiting for transfers between devices, shards(): parts = lax.all_to_all(ready, 'lon', 0, 0, axis_index_groups=cores)  8.11 us
    pallas_call x1, Pallas kernels, shards(): call(behind_kernel, 6, grid=(2,), in_specs=[half, half] + [fixed(r.shape)...  6.73 us
    pallas_call x1, Pallas kernels, shards(): call(back_b_kernel, 4, out_shape=[shaped(*s) for s in (b, b, edge, edge)])  4.95 us
    all_to_all x1, starting transfers between devices, shards(): part = lax.all_to_all(part, 'lat', 0, 0).astype(f32).sum(0)  4.84 us
  transfers between devices with their start and end apart: 15, of which 2 were waited for; matrix products, arithmetic and copies ran while one was open for 1% of the time, Pallas kernels for 43%

profile of v1, /device:TPU:1, one launch (start us, length us, event | category | flops | bytes accessed | tf_op | source)
XLA Modules:
  0.0 121.8 jit_solution(9569168615050044327)
XLA Ops:
  0.6 3.7 %shard_map.147 = (bf16[2,304,512]{2,1,0:T(8,128)(2,1)}, bf16[2,288,512]{2,1,0:T(8,128)(2,1)}) custom-call(bf16[2,12,48,512]{3,2,1,0:T(8,128)(2,1)} %x_ref.3, bf16[2,12,48,512]{3,2,1,0:T(8,128)(2,1)} %g_ref.3, s32[12,48]{1,0:T(8,128)} %regions_ref.1, bf16[288,384]{1,0:T(8,128)(2,1)} %constant.38.clone.place_ref), custom_call_target="tpu_custom_call" | custom-call | flops 3000000000 | bytes 1024 | tf_op jit(solution)/shard_map/pallas_call | solution.py:529
  4.3 3.6 %collective-permute-start = (bf16[2,304,512]{2,1,0:T(8,128)(2,1)}, bf16[2,304,512]{2,1,0:T(8,128)(2,1)S(1)}, u32[]{:S(2)}, u32[]{:S(2)}) collective-permute-start(bf16[2,304,512]{2,1,0:T(8,128)(2,1)} %get-tuple-element.45), channel_id=1, source_target_pairs={{0,16},{1,17},{2,18},{3,19},{4,20},{5,21},{6,22},{7,23},{8,24},{9,... | collective-permute-start | bytes 1867784 | tf_op jit(solution)/shard_map/ppermute | solution.py:397
  7.9 7.5 %collective-permute-start.1 = (bf16[2,288,512]{2,1,0:T(8,128)(2,1)}, bf16[2,288,512]{2,1,0:T(8,128)(2,1)S(1)}, u32[]{:S(2)}, u32[]{:S(2)}) collective-permute-start(bf16[2,288,512]{2,1,0:T(8,128)(2,1)} %get-tuple-element.46), channel_id=1, source_target_pairs={{0,224},{1,225},{2,226},{3,227},{4,228},{5,229},{6,230},{7,231},{8... | collective-permute-start | bytes 1769480 | tf_op jit(solution)/shard_map/ppermute | solution.py:397
  15.4 4.4 %shard_map.148 = (bf16[2,224,512]{2,1,0:T(8,128)(2,1)}, bf16[2,224,512]{2,1,0:T(8,128)(2,1)}, bf16[2,80,512]{2,1,0:T(8,128)(2,1)}, bf16[2,80,512]{2,1,0:T(8,128)(2,1)}) custom-call(bf16[2,12,48,512]{3,2,1,0:T(8,128)(2,1)} %x_ref.3, bf16[2,12,48,512]{3,2,1,0:T(8,128)(2,1)} %g_ref.3, bf16[224,576]{1,0:T(8,128)(2,1)} %constant.39.clone.place_ref, ...), custom_call_target="tpu_custom_call" | custom-call | flops 5000000000 | bytes 1024 | tf_op jit(solution)/shard_map/pallas_call | solution.py:540
  19.8 0.0 collective-permute-start.2
  19.8 2.6 %collective-permute-start.3 = (bf16[2,224,512]{2,1,0:T(8,128)(2,1)}, bf16[2,224,512]{2,1,0:T(8,128)(2,1)}, u32[]{:S(2)}, u32[]{:S(2)}) collective-permute-start(bf16[2,224,512]{2,1,0:T(8,128)(2,1)} %get-tuple-element.48), channel_id=1, source_target_pairs={{0,224},{1,225},{2,226},{3,227},{4,228},{5,229},{6,230},{7,231},{8... | collective-permute-start | bytes 1376264 | tf_op jit(solution)/shard_map/ppermute | solution.py:397
  22.4 6.8 %collective-permute-start.4 = (bf16[2,80,512]{2,1,0:T(8,128)(2,1)}, bf16[2,80,512]{2,1,0:T(8,128)(2,1)S(1)}, u32[]{:S(2)}, u32[]{:S(2)}) collective-permute-start(bf16[2,80,512]{2,1,0:T(8,128)(2,1)} %get-tuple-element.49), channel_id=1, source_target_pairs={{0,31},{1,16},{2,17},{3,18},{4,19},{5,20},{6,21},{7,22},{8,23},{9,... | collective-permute-start | bytes 491528 | tf_op jit(solution)/shard_map/ppermute | solution.py:397
  29.2 0.0 collective-permute-done.1.lo.loa
  29.2 4.7 %collective-permute-start.5 = (bf16[2,80,512]{2,1,0:T(8,128)(2,1)}, bf16[2,80,512]{2,1,0:T(8,128)(2,1)S(1)}, u32[]{:S(2)}, u32[]{:S(2)}) collective-permute-start(bf16[2,80,512]{2,1,0:T(8,128)(2,1)} %get-tuple-element.50), channel_id=1, source_target_pairs={{0,239},{1,224},{2,225},{3,226},{4,227},{5,228},{6,229},{7,230},{8... | collective-permute-start | bytes 491528 | tf_op jit(solution)/shard_map/ppermute | solution.py:397
  33.9 0.0 collective-permute-done.up.upa
  33.9 0.0 copy-done.5
  33.9 0.8 copy-done.2
  34.7 13.7 %shard_map.149 = (bf16[2,576,256]{2,1,0:T(8,128)(2,1)}, bf16[2,3,576,256]{3,2,1,0:T(8,128)(2,1)}, bf16[2,288,512]{2,1,0:T(8,128)(2,1)}, bf16[2,288,512]{2,1,0:T(8,128)(2,1)}) custom-call(bf16[2,304,512]{2,1,0:T(8,128)(2,1)} %copy-done.2, bf16[2,288,512]{2,1,0:T(8,128)(2,1)} %copy-done.5, bf16[512,1536]{1,0:T(8,128)(2,1)} %wqkv_ref.1, bf16[512,512]{1,0:T(8,128)(2,1)} %wout_ref.1), custom_call_target="tpu_custom_call" | custom-call | flops 12999999488 | bytes 1024 | tf_op jit(solution)/shard_map/pallas_call | solution.py:474
  48.4 0.1 collective-permute-start.6
  48.5 0.0 collective-permute-done.4.eup
  48.5 0.0 copy-start.11
  48.5 2.1 %collective-permute-start.7 = (bf16[2,288,512]{2,1,0:T(8,128)(2,1)}, bf16[2,288,512]{2,1,0:T(8,128)(2,1)S(1)}, u32[]{:S(2)}, u32[]{:S(2)}) collective-permute-start(bf16[2,288,512]{2,1,0:T(8,128)(2,1)} %get-tuple-element.60), channel_id=1, source_target_pairs={{224,0},{225,1},{226,2},{227,3},{228,4},{229,5},{230,6},{231,7},{2... | collective-permute-start | bytes 1769480 | tf_op jit(solution)/shard_map/ppermute | solution.py:406
  50.7 0.0 collective-permute-done.5.elo
  50.7 0.0 copy-start.14
  50.7 0.0 collective-permute-done.2.up
  50.7 0.0 copy-start.6
  50.7 0.0 collective-permute-done.3.lo
  50.7 0.0 copy-done.11
  50.7 0.6 copy-done.14
  51.3 0.2 copy-done.6
  51.5 20.9 %shard_map.150 = (bf16[2,576,256]{2,1,0:T(8,128)(2,1)}, bf16[2,3,576,256]{3,2,1,0:T(8,128)(2,1)}, bf16[8,128,512]{2,1,0:T(8,128)(2,1)}, bf16[8,128,512]{2,1,0:T(8,128)(2,1)}) custom-call(s32[1]{0:T(128)} %bitcast.core_ref, bf16[2,304,512]{2,1,0:T(8,128)(2,1)} %copy-done.2, bf16[2,288,512]{2,1,0:T(8,128)(2,1)} %copy-done.5, bf16[2,224,512]{2,1,0:T(8,128)(2,1)} %copy-done.6, ...), custom_call_target="tpu_custom_call" | custom-call | flops 17999998976 | bytes 1024 | tf_op jit(solution)/shard_map/pallas_call | solution.py:494
  72.4 0.0 collective-permute-done.6.upa_ref
  72.4 0.0 copy-start.3
  72.4 0.0 collective-permute-done.7.loa_ref
  72.4 0.0 copy-start.4
  72.4 0.1 collective-permute-start.8
  72.5 0.0 copy-start
  72.6 4.9 %shard_map.151 = (bf16[2,224,512]{2,1,0:T(8,128)(2,1)}, bf16[2,224,512]{2,1,0:T(8,128)(2,1)}, bf16[2,80,512]{2,1,0:T(8,128)(2,1)}, bf16[2,80,512]{2,1,0:T(8,128)(2,1)}) custom-call(bf16[2,576,256]{2,1,0:T(8,128)(2,1)} %get-tuple-element.65.att_ref, bf16[2,3,576,256]{3,2,1,0:T(8,128)(2,1)} %get-tuple-element.66.rows_ref, bf16[512,1536]{1,0:T(8,128)(2,1)} %wqkv_ref.1, ...), custom_call_target="tpu_custom_call" | custom-call | flops 4000000000 | bytes 1024 | tf_op jit(solution)/shard_map/pallas_call | solution.py:559
  77.5 0.0 copy-done.3
  77.5 0.0 copy-done.4
  77.5 0.0 collective-permute-done.8
  77.5 0.0 copy-done
  77.5 1.3 %add_convert_fusion = bf16[8,128,512]{2,1,0:T(8,128)(2,1)} fusion(bf16[8,128,512]{2,1,0:T(8,128)(2,1)S(1)} %collective-permute-done.8, bf16[8,128,512]{2,1,0:T(8,128)(2,1)S(1)} %copy-done), kind=kLoop, calls=%fused_computation | loop fusion | flops 2097152 | bytes 3145728 | tf_op jit(solution)/shard_map/convert_element_type | solution.py:562
  78.8 4.4 %all-to-all-start = ((bf16[8,128,512]{2,1,0:T(8,128)(2,1)}), bf16[8,128,512]{2,1,0:T(8,128)(2,1)S(1)}, u32[]{:S(2)}, u32[]{:S(2)}) async-start(bf16[8,128,512]{2,1,0:T(8,128)(2,1)} %add_convert_fusion), calls=%async_computation | async-start | bytes 2097152 | tf_op jit(solution)/shard_map/all_to_all | solution.py:565
  83.2 0.0 copy-done.8
  83.2 1.9 %collective-permute-start.10 = (bf16[2,224,512]{2,1,0:T(8,128)(2,1)S(1)}, bf16[2,224,512]{2,1,0:T(8,128)(2,1)S(1)}, u32[]{:S(2)}, u32[]{:S(2)}) collective-permute-start(bf16[2,224,512]{2,1,0:T(8,128)(2,1)S(1)} %copy-done.8), channel_id=1, source_target_pairs={{224,0},{225,1},{226,2},{227,3},{228,4},{229,5},{230,6},{231,7},{2... | collective-permute-start | bytes 1376264 | tf_op jit(solution)/shard_map/ppermute | solution.py:406
  85.1 0.0 copy-done.7
  85.1 2.0 %collective-permute-start.9 = (bf16[2,224,512]{2,1,0:T(8,128)(2,1)S(1)}, bf16[2,224,512]{2,1,0:T(8,128)(2,1)S(1)}, u32[]{:S(2)}, u32[]{:S(2)}) collective-permute-start(bf16[2,224,512]{2,1,0:T(8,128)(2,1)S(1)} %copy-done.7), channel_id=1, source_target_pairs={{16,0},{17,1},{18,2},{19,3},{20,4},{21,5},{22,6},{23,7},{24,8},{25... | collective-permute-start | bytes 1376264 | tf_op jit(solution)/shard_map/ppermute | solution.py:406
  87.1 1.4 %dynamic-slice_bitcast_fusion.by_ref = bf16[128,128]{1,0:T(8,128)(2,1)} fusion(bf16[16,128,128]{2,1,0:T(8,128)(2,1)} %constant.42.clone, s32[]{:T(128)S(6)} %select_n.11), kind=kLoop, calls=%fused_computation.2 | loop fusion | bytes 65540 | tf_op jit(solution)/shard_map/squeeze | solution.py:579
  88.5 0.0 copy-done.13
  88.5 3.0 %collective-permute-start.11 = (bf16[2,80,512]{2,1,0:T(8,128)(2,1)S(1)}, bf16[2,80,512]{2,1,0:T(8,128)(2,1)S(1)}, u32[]{:S(2)}, u32[]{:S(2)}) collective-permute-start(bf16[2,80,512]{2,1,0:T(8,128)(2,1)S(1)} %copy-done.13), channel_id=1, source_target_pairs={{31,0},{16,1},{17,2},{18,3},{19,4},{20,5},{21,6},{22,7},{23,8},{24... | collective-permute-start | bytes 491528 | tf_op jit(solution)/shard_map/ppermute | solution.py:406
  91.4 0.0 copy-done.12
  91.4 0.0 collective-permute-start.12
  91.4 8.1 %all-to-all-done.parts_ref = bf16[8,128,512]{2,1,0:T(8,128)(2,1)S(1)} async-done(((bf16[8,128,512]{2,1,0:T(8,128)(2,1)}), bf16[8,128,512]{2,1,0:T(8,128)(2,1)S(1)}, u32[]{:S(2)}, u32[]{:S(2)}) %all-to-all-start) | async-done | bytes 1048608 | tf_op jit(solution)/shard_map/all_to_all | solution.py:565
  99.5 1.0 copy-done.1
  100.5 2.2 %shard_map.153 = bf16[16,8,512]{2,1,0:T(8,128)(2,1)} custom-call(bf16[8,128,512]{2,1,0:T(8,128)(2,1)} %copy-done.1, bf16[128,128]{1,0:T(8,128)(2,1)} %dynamic-slice_bitcast_fusion.by_ref), custom_call_target="tpu_custom_call" | custom-call | flops 2000000000 | bytes 1024 | tf_op jit(solution)/shard_map/pallas_call | solution.py:580
  102.7 4.8 %all-to-all-start.1 = ((bf16[16,8,512]{2,1,0:T(8,128)(2,1)}), bf16[16,8,512]{2,1,0:T(8,128)(2,1)S(1)}, u32[]{:S(2)}, u32[]{:S(2)}) async-start(bf16[16,8,512]{2,1,0:T(8,128)(2,1)} %shard_map.153), calls=%async_computation.1 | async-start | bytes 262144 | tf_op jit(solution)/shard_map/all_to_all | solution.py:581
  107.5 4.7 %collective-permute-done.11.eup_ref = bf16[2,80,512]{2,1,0:T(8,128)(2,1)S(1)} collective-permute-done((bf16[2,80,512]{2,1,0:T(8,128)(2,1)S(1)}, bf16[2,80,512]{2,1,0:T(8,128)(2,1)S(1)}, u32[]{:S(2)}, u32[]{:S(2)}) %collective-permute-start.11) | collective-permute-done | bytes 163872 | tf_op jit(solution)/shard_map/ppermute | solution.py:406
  112.2 0.0 collective-permute-done.12.elo_ref
  112.2 0.0 collective-permute-done.10.lob_ref
  112.2 0.0 collective-permute-done.9.upb_ref
  112.2 0.6 copy-done.15
  112.8 0.1 copy-done.16
  112.9 0.2 copy-done.9
  113.1 0.8 copy-done.10
  113.9 6.7 %shard_map.152 = (bf16[2,12,48,512]{3,2,1,0:T(8,128)(2,1)}, bf16[2,12,48,512]{3,2,1,0:T(8,128)(2,1)}) custom-call(bf16[2,12,48,512]{3,2,1,0:T(8,128)(2,1)} %x_ref.3, bf16[2,12,48,512]{3,2,1,0:T(8,128)(2,1)} %g_ref.3, bf16[2,288,512]{2,1,0:T(8,128)(2,1)} %copy-done.3, bf16[2,288,512]{2,1,0:T(8,128)(2,1)} %copy-done.4, bf16[2,224,512]{2,1,0:T(8,128)(2,1)} %copy-done.10, ...), custom_call_target="tpu_custom_call" | custom-call | flops 6000000000 | bytes 1024 | tf_op jit(solution)/shard_map/pallas_call | solution.py:570
  120.6 0.0 all-to-all-done.1
  120.6 0.6 slice_bitcast_fusion
  121.2 0.6 slice_bitcast_fusion.1
  (12 shorter events, 0.0 us)
Async XLA Ops:
  4.3 29.6 %collective-permute-start = (bf16[2,304,512]{2,1,0:T(8,128)(2,1)}, bf16[2,304,512]{2,1,0:T(8,128)(2,1)S(1)}, u32[]{:S(2)}, u32[]{:S(2)}) collective-permute-start(bf16[2,304,512]{2,1,0:T(8,128)(2,1)} %get-tuple-element.45), channel_id=1, source_target_pairs={{0,16},{1,17},{2,18},{3,19},{4,20},{5,21},{6,22},{7,23},{8,24},{9,... | collective-permute-start | bytes 1867784 | tf_op jit(solution)/shard_map/ppermute | solution.py:397
  7.9 21.3 %collective-permute-start.1 = (bf16[2,288,512]{2,1,0:T(8,128)(2,1)}, bf16[2,288,512]{2,1,0:T(8,128)(2,1)S(1)}, u32[]{:S(2)}, u32[]{:S(2)}) collective-permute-start(bf16[2,288,512]{2,1,0:T(8,128)(2,1)} %get-tuple-element.46), channel_id=1, source_target_pairs={{0,224},{1,225},{2,226},{3,227},{4,228},{5,229},{6,230},{7,231},{8... | collective-permute-start | bytes 1769480 | tf_op jit(solution)/shard_map/ppermute | solution.py:397
  19.8 30.9 %collective-permute-start.2 = (bf16[2,224,512]{2,1,0:T(8,128)(2,1)}, bf16[2,224,512]{2,1,0:T(8,128)(2,1)S(1)}, u32[]{:S(2)}, u32[]{:S(2)}) collective-permute-start(bf16[2,224,512]{2,1,0:T(8,128)(2,1)} %get-tuple-element.47), channel_id=1, source_target_pairs={{0,16},{1,17},{2,18},{3,19},{4,20},{5,21},{6,22},{7,23},{8,24},{9,... | collective-permute-start | bytes 1376264 | tf_op jit(solution)/shard_map/ppermute | solution.py:397
  19.8 30.9 %collective-permute-start.3 = (bf16[2,224,512]{2,1,0:T(8,128)(2,1)}, bf16[2,224,512]{2,1,0:T(8,128)(2,1)}, u32[]{:S(2)}, u32[]{:S(2)}) collective-permute-start(bf16[2,224,512]{2,1,0:T(8,128)(2,1)} %get-tuple-element.48), channel_id=1, source_target_pairs={{0,224},{1,225},{2,226},{3,227},{4,228},{5,229},{6,230},{7,231},{8... | collective-permute-start | bytes 1376264 | tf_op jit(solution)/shard_map/ppermute | solution.py:397
  22.4 26.1 %collective-permute-start.4 = (bf16[2,80,512]{2,1,0:T(8,128)(2,1)}, bf16[2,80,512]{2,1,0:T(8,128)(2,1)S(1)}, u32[]{:S(2)}, u32[]{:S(2)}) collective-permute-start(bf16[2,80,512]{2,1,0:T(8,128)(2,1)} %get-tuple-element.49), channel_id=1, source_target_pairs={{0,31},{1,16},{2,17},{3,18},{4,19},{5,20},{6,21},{7,22},{8,23},{9,... | collective-permute-start | bytes 491528 | tf_op jit(solution)/shard_map/ppermute | solution.py:397
  29.2 4.7 %copy-start.5 = (bf16[2,288,512]{2,1,0:T(8,128)(2,1)}, bf16[2,288,512]{2,1,0:T(8,128)(2,1)S(1)}, u32[]{:S(2)}) copy-start(bf16[2,288,512]{2,1,0:T(8,128)(2,1)S(1)} %collective-permute-done.1.lo.loa) | copy-start | bytes 1769476
  29.2 21.5 %collective-permute-start.5 = (bf16[2,80,512]{2,1,0:T(8,128)(2,1)}, bf16[2,80,512]{2,1,0:T(8,128)(2,1)S(1)}, u32[]{:S(2)}, u32[]{:S(2)}) collective-permute-start(bf16[2,80,512]{2,1,0:T(8,128)(2,1)} %get-tuple-element.50), channel_id=1, source_target_pairs={{0,239},{1,224},{2,225},{3,226},{4,227},{5,228},{6,229},{7,230},{8... | collective-permute-start | bytes 491528 | tf_op jit(solution)/shard_map/ppermute | solution.py:397
  33.9 0.8 copy-start.2
  48.4 24.0 %collective-permute-start.6 = (bf16[2,288,512]{2,1,0:T(8,128)(2,1)}, bf16[2,288,512]{2,1,0:T(8,128)(2,1)S(1)}, u32[]{:S(2)}, u32[]{:S(2)}) collective-permute-start(bf16[2,288,512]{2,1,0:T(8,128)(2,1)} %get-tuple-element.59), channel_id=1, source_target_pairs={{16,0},{17,1},{18,2},{19,3},{20,4},{21,5},{22,6},{23,7},{24,8},{25... | collective-permute-start | bytes 1769480 | tf_op jit(solution)/shard_map/ppermute | solution.py:406
  48.5 2.2 %copy-start.11 = (bf16[2,80,512]{2,1,0:T(8,128)(2,1)}, bf16[2,80,512]{2,1,0:T(8,128)(2,1)S(1)}, u32[]{:S(2)}) copy-start(bf16[2,80,512]{2,1,0:T(8,128)(2,1)S(1)} %collective-permute-done.4.eup) | copy-start | bytes 491524
  48.5 23.9 %collective-permute-start.7 = (bf16[2,288,512]{2,1,0:T(8,128)(2,1)}, bf16[2,288,512]{2,1,0:T(8,128)(2,1)S(1)}, u32[]{:S(2)}, u32[]{:S(2)}) collective-permute-start(bf16[2,288,512]{2,1,0:T(8,128)(2,1)} %get-tuple-element.60), channel_id=1, source_target_pairs={{224,0},{225,1},{226,2},{227,3},{228,4},{229,5},{230,6},{231,7},{2... | collective-permute-start | bytes 1769480 | tf_op jit(solution)/shard_map/ppermute | solution.py:406
  50.7 0.7 copy-start.14
  50.7 0.8 copy-start.6
  72.4 5.1 %copy-start.3 = (bf16[2,288,512]{2,1,0:T(8,128)(2,1)}, bf16[2,288,512]{2,1,0:T(8,128)(2,1)S(1)}, u32[]{:S(2)}) copy-start(bf16[2,288,512]{2,1,0:T(8,128)(2,1)S(1)} %collective-permute-done.6.upa_ref) | copy-start | bytes 1769476
  72.4 5.1 %copy-start.4 = (bf16[2,288,512]{2,1,0:T(8,128)(2,1)}, bf16[2,288,512]{2,1,0:T(8,128)(2,1)S(1)}, u32[]{:S(2)}) copy-start(bf16[2,288,512]{2,1,0:T(8,128)(2,1)S(1)} %collective-permute-done.7.loa_ref) | copy-start | bytes 1769476
  72.4 5.1 %collective-permute-start.8 = (bf16[8,128,512]{2,1,0:T(8,128)(2,1)}, bf16[8,128,512]{2,1,0:T(8,128)(2,1)S(1)}, u32[]{:S(2)}, u32[]{:S(2)}) collective-permute-start(bf16[8,128,512]{2,1,0:T(8,128)(2,1)} %get-tuple-element.64), channel_id=1, source_target_pairs={{0,1},{1,0},{2,3},{3,2},{4,5},{5,4},{6,7},{7,6},{8,9},{9,8},{10,11... | collective-permute-start | bytes 3145736 | tf_op jit(solution)/shard_map/ppermute | solution.py:397
  72.5 5.0 %copy-start = (bf16[8,128,512]{2,1,0:T(8,128)(2,1)S(1)}, bf16[8,128,512]{2,1,0:T(8,128)(2,1)}, u32[]{:S(2)}) copy-start(bf16[8,128,512]{2,1,0:T(8,128)(2,1)} %get-tuple-element.63) | copy-start | bytes 3145732
  78.8 4.4 %copy-start.8 = (bf16[2,224,512]{2,1,0:T(8,128)(2,1)S(1)}, bf16[2,224,512]{2,1,0:T(8,128)(2,1)}, u32[]{:S(2)}) copy-start(bf16[2,224,512]{2,1,0:T(8,128)(2,1)} %get-tuple-element.72) | copy-start | bytes 1376260
  78.8 6.3 %copy-start.7 = (bf16[2,224,512]{2,1,0:T(8,128)(2,1)S(1)}, bf16[2,224,512]{2,1,0:T(8,128)(2,1)}, u32[]{:S(2)}) copy-start(bf16[2,224,512]{2,1,0:T(8,128)(2,1)} %get-tuple-element.71) | copy-start | bytes 1376260
  78.8 9.6 %copy-start.13 = (bf16[2,80,512]{2,1,0:T(8,128)(2,1)S(1)}, bf16[2,80,512]{2,1,0:T(8,128)(2,1)}, u32[]{:S(2)}) copy-start(bf16[2,80,512]{2,1,0:T(8,128)(2,1)} %get-tuple-element.73) | copy-start | bytes 491524
  78.8 12.6 %copy-start.12 = (bf16[2,80,512]{2,1,0:T(8,128)(2,1)S(1)}, bf16[2,80,512]{2,1,0:T(8,128)(2,1)}, u32[]{:S(2)}) copy-start(bf16[2,80,512]{2,1,0:T(8,128)(2,1)} %get-tuple-element.74) | copy-start | bytes 491524
  78.8 20.7 %all-to-all-start = ((bf16[8,128,512]{2,1,0:T(8,128)(2,1)}), bf16[8,128,512]{2,1,0:T(8,128)(2,1)S(1)}, u32[]{:S(2)}, u32[]{:S(2)}) async-start(bf16[8,128,512]{2,1,0:T(8,128)(2,1)} %add_convert_fusion), calls=%async_computation | async-start | bytes 2097152 | tf_op jit(solution)/shard_map/all_to_all | solution.py:565
  83.2 29.0 %collective-permute-start.10 = (bf16[2,224,512]{2,1,0:T(8,128)(2,1)S(1)}, bf16[2,224,512]{2,1,0:T(8,128)(2,1)S(1)}, u32[]{:S(2)}, u32[]{:S(2)}) collective-permute-start(bf16[2,224,512]{2,1,0:T(8,128)(2,1)S(1)} %copy-done.8), channel_id=1, source_target_pairs={{224,0},{225,1},{226,2},{227,3},{228,4},{229,5},{230,6},{231,7},{2... | collective-permute-start | bytes 1376264 | tf_op jit(solution)/shard_map/ppermute | solution.py:406
  85.1 27.1 %collective-permute-start.9 = (bf16[2,224,512]{2,1,0:T(8,128)(2,1)S(1)}, bf16[2,224,512]{2,1,0:T(8,128)(2,1)S(1)}, u32[]{:S(2)}, u32[]{:S(2)}) collective-permute-start(bf16[2,224,512]{2,1,0:T(8,128)(2,1)S(1)} %copy-done.7), channel_id=1, source_target_pairs={{16,0},{17,1},{18,2},{19,3},{20,4},{21,5},{22,6},{23,7},{24,8},{25... | collective-permute-start | bytes 1376264 | tf_op jit(solution)/shard_map/ppermute | solution.py:406
  88.5 23.7 %collective-permute-start.11 = (bf16[2,80,512]{2,1,0:T(8,128)(2,1)S(1)}, bf16[2,80,512]{2,1,0:T(8,128)(2,1)S(1)}, u32[]{:S(2)}, u32[]{:S(2)}) collective-permute-start(bf16[2,80,512]{2,1,0:T(8,128)(2,1)S(1)} %copy-done.13), channel_id=1, source_target_pairs={{31,0},{16,1},{17,2},{18,3},{19,4},{20,5},{21,6},{22,7},{23,8},{24... | collective-permute-start | bytes 491528 | tf_op jit(solution)/shard_map/ppermute | solution.py:406
  91.4 20.8 %collective-permute-start.12 = (bf16[2,80,512]{2,1,0:T(8,128)(2,1)S(1)}, bf16[2,80,512]{2,1,0:T(8,128)(2,1)S(1)}, u32[]{:S(2)}, u32[]{:S(2)}) collective-permute-start(bf16[2,80,512]{2,1,0:T(8,128)(2,1)S(1)} %copy-done.12), channel_id=1, source_target_pairs={{239,0},{224,1},{225,2},{226,3},{227,4},{228,5},{229,6},{230,7},{2... | collective-permute-start | bytes 491528 | tf_op jit(solution)/shard_map/ppermute | solution.py:406
  99.5 1.0 copy-start.1
  102.7 17.9 %all-to-all-start.1 = ((bf16[16,8,512]{2,1,0:T(8,128)(2,1)}), bf16[16,8,512]{2,1,0:T(8,128)(2,1)S(1)}, u32[]{:S(2)}, u32[]{:S(2)}) async-start(bf16[16,8,512]{2,1,0:T(8,128)(2,1)} %shard_map.153), calls=%async_computation.1 | async-start | bytes 262144 | tf_op jit(solution)/shard_map/all_to_all | solution.py:581
  112.2 0.7 copy-start.15
  112.2 0.7 copy-start.16
  112.2 0.9 copy-start.9
  113.1 0.8 copy-start.10

commit v2 on v1

--- a/solution.py
+++ b/solution.py
@@ -29,6 +29,7 @@
 SPLIT = CHUNK * TOK
 LOG2E = 1.4426950408889634
 VMEM = 60 * 1024 * 1024
+MOST = 63 * 1024 * 1024 + 512 * 1024
 NT = (((1,), (1,)), ((), ()))
 TN = (((0,), (0,)), ((), ()))
 f32, bf16 = jnp.float32, jnp.bfloat16
@@ -63,34 +64,37 @@
     return early, late, place, cut
 
 
+def split(lat, lon):
+    core, y, last = lon % 2, lon // 4, lat // 2 % 2
+    within = (lat // 4 * 2 + lat % 2) * 2 + lon // 2 % 2
+    return core, last * 4 + y, within
+
+
 def orders():
-    by_lon = np.zeros((2, GROUPS, LONS * GW, 3 * QUAD), np.float32)
-    out_by_lon = np.zeros((2, D, D), np.float32)
-    by_lat = np.zeros((LONS, LATS * 8, LATS * 8), np.float32)
-
-    def place(core, lon):
-        return (lon % 2 ^ core) * LONS // 2 + lon // 2
-
+    by_class = np.zeros((2, GROUPS, LONS * GW, 3 * QUAD), np.float32)
+    out_by_class = np.zeros((2, D, D), np.float32)
+    by_place = np.zeros((LONS, LATS * 8, LATS * 8), np.float32)
     for group in range(GROUPS):
-        filled = [0] * LONS
+        filled = np.zeros((2, LONS // 2), np.int64)
         for row in range(3 * QUAD):
             column = row // QUAD * D + group * QUAD + row % QUAD
             device, at = divmod(column, SPAN)
-            lat, lon = divmod(device, LONS)
-            for core in range(2):
-                by_lon[core, group, place(core, lon) * GW + filled[lon], row] = 1
-            by_lat[lon, lat * 8 + at, group * GW + filled[lon]] = 1
-            filled[lon] += 1
-        assert filled == [GW] * LONS
+            core, rest, within = split(*divmod(device, LONS))
+            slot = filled[core, rest]
+            for mine in range(2):
+                to = ((core ^ mine) * LONS // 2 + rest) * GW + slot
+                by_class[mine, group, to, row] = 1
+            by_place[core * LONS // 2 + rest, within * 8 + at, group * GW + slot] = 1
+            filled[core, rest] += 1
+        assert (filled == GW).all()
     for row in range(D):
         device, at = divmod(row, SPAN_OUT)
-        lat, lon = divmod(device, LONS)
-        for core in range(2):
-            out_by_lon[core, place(core, lon) * GO + lat * SPAN_OUT + at, row] = 1
-    for lat in range(LATS):
-        for at in range(SPAN_OUT):
-            by_lat[:, lat * 8 + SPAN + at, GROUPS * GW + lat * SPAN_OUT + at] = 1
-    return by_lon, out_by_lon, by_lat
+        core, rest, within = split(*divmod(device, LONS))
+        slot = within * SPAN_OUT + at
+        for mine in range(2):
+            out_by_class[mine, ((core ^ mine) * LONS // 2 + rest) * GO + slot, row] = 1
+        by_place[core * LONS // 2 + rest, within * 8 + SPAN + at, GROUPS * GW + slot] = 1
+    return by_class, out_by_class, by_place
 
 
 EARLY_PLACE, LATE_PLACE, PLACE, CUT = one_hots()
@@ -199,11 +203,11 @@
         if part == 0:
             att_s[group, rows] = pick(mm(p_s[w], v_s[rows], TN))
         elif part == 1:
-            rows_s[group, 0, rows] = pick(mm(ds_s[w], k_s[rows], TN))
+            rows_s[group, rows, 0:256] = pick(mm(ds_s[w], k_s[rows], TN))
         elif part == 2:
-            rows_s[group, 1, rows] = mm(ds_s[w], qs_s[w]).astype(bf16)
+            rows_s[group, rows, 256:512] = mm(ds_s[w], qs_s[w]).astype(bf16)
         else:
-            rows_s[group, 2, rows] = mm(p_s[w], gs_s[w]).astype(bf16)
+            rows_s[group, rows, 512:768] = mm(p_s[w], gs_s[w]).astype(bf16)
 
     wide = HPG * WTOK
     tiles = [slice(i, min(i + 256, wide)) for i in range(0, wide, 256)]
@@ -265,11 +269,11 @@
 
 def chunk_b_kernel(
     core_ref, upa, loa, up, lo, eup, elo, wqkv, wout, atta, rowsa, by_lon, out_by_lon,
-    att, rows, mine, theirs, *refs,
+    mine, theirs, rup, rlo, reup, relo, *refs,
 ):
     x_s, g_s, flag_s, wqkv_s, wout_s, att_s, rows_s, in_sems, out_sems, late_sems = refs[:10]
-    here_s, there_s, xa_s, ga_s, atta_s, rowsa_s, by_s, out_by_s, o_s = refs[10:19]
-    scratch = refs[19:]
+    here_s, there_s, xa_s, ga_s, atta_s, rowsa_s, by_s, out_by_s, o_s, rup_s, rlo_s, reup_s, relo_s = refs[10:23]
+    scratch = refs[23:]
     core = core_ref[0]
     last = pl.ds((CHUNK - 1) * TOK, RIMP)
     copies = starts(
@@ -305,23 +309,20 @@
             to = (CHUNK - 1) * WTOK + half * TOK
             dst[to : to + TOK] = jnp.concatenate([here, there], axis=0).astype(bf16)
     flags = flag_s[...].astype(f32)[0:1]
-    outs = []
     for group in range(GROUPS):
         attend(flags, CHUNK, group, x_s, g_s, wqkv_s, wout_s, att_s, rows_s, scratch)
-        pairs = [(att_s.at[group], att.at[group]), (rows_s.at[group], rows.at[group])]
-        outs += starts(pairs, out_sems.at[pl.ds(2 * group, 2)])
         if group == 0:
             waits(late)
-        parts = []
-        for i in range(3):
-            total = mm(rowsa_s[group, i], xa_s[...], TN) + mm(rows_s[group, i], x_s[...], TN)
-            parts.append(total.astype(bf16))
-        ready = move(by_s[group], jnp.concatenate(parts, axis=0))
+        total = mm(xa_s[...], rowsa_s[group], TN) + mm(x_s[...], rows_s[group], TN)
+        ready = mm(by_s[group], total.astype(bf16), NT).astype(bf16)
         o_s[:, :, group * GW : (group + 1) * GW] = ready.reshape(2, LONS // 2, GW, D)
-        out = (mm(ga_s[...], atta_s[group], TN) + mm(g_s[...], att_s[group], TN)).astype(bf16)
-        out = move(out_by_s[...], out).reshape(2, LONS // 2, GO, QUAD)
+        out = (mm(atta_s[group], ga_s[...], TN) + mm(att_s[group], g_s[...], TN)).astype(bf16)
+        out = mm(out_by_s[...], out, NT).astype(bf16).reshape(2, LONS // 2, GO, QUAD)
         o_s[:, :, GROUPS * GW :, group * QUAD : (group + 1) * QUAD] = out
-    outs += starts([(o_s.at[0], mine), (o_s.at[1], theirs)], out_sems.at[pl.ds(2 * GROUPS, 2)])
+    outs = starts([(o_s.at[0], mine), (o_s.at[1], theirs)], out_sems.at[pl.ds(0, 2)])
+    back(True, att_s, rows_s, wqkv_s, wout_s, rup_s, rlo_s, reup_s, relo_s)
+    pairs = [(rup_s, rup), (rlo_s, rlo), (reup_s, reup), (relo_s, relo)]
+    outs += starts(pairs, out_sems.at[pl.ds(2, 4)])
     waits(outs)
 
 
@@ -333,7 +334,7 @@
             branch = branch + mm(att_s[i, rows], wout_s[QUAD * i : QUAD * (i + 1)])
             for j in range(3):
                 at = D * j + QUAD * i
-                gn = gn + mm(rows_s[i, j, rows], wqkv_s[:, at : at + QUAD], NT)
+                gn = gn + mm(rows_s[i, rows, QUAD * j : QUAD * (j + 1)], wqkv_s[:, at : at + QUAD], NT)
         for at, full in enumerate((branch, gn)):
             for half, dst in enumerate((up_ref, lo_ref)):
                 part = full[half * TOK : (half + 1) * TOK]
@@ -343,10 +344,6 @@
                     edges[half][at] = jnp.concatenate([part[RIM:], pad], axis=0).astype(bf16)
                 else:
                     dst[at, w * TOK : (w + 1) * TOK] = part.astype(bf16)
-
-
-def back_b_kernel(att_ref, rows_ref, wqkv_ref, wout_ref, *outs):
-    back(True, att_ref, rows_ref, wqkv_ref, wout_ref, *outs)
 
 
 def behind_kernel(
@@ -388,6 +385,14 @@
     o_ref[...] = move(by_ref[...], total.astype(bf16)).reshape(LATS, 8, D)
 
 
+def last_kernel(parts_ref, qkv_ref, out_ref):
+    total = parts_ref[0].astype(f32)
+    for i in range(1, LATS):
+        total = total + parts_ref[i].astype(f32)
+    qkv_ref[...] = total[:SPAN]
+    out_ref[...] = total[SPAN:]
+
+
 def send(x, place):
     pairs = []
     for i in range(LATS):
@@ -426,9 +431,9 @@
     return jax.ShapeDtypeStruct(shape, dtype)
 
 
-def call(kernel, us, **kwargs):
+def call(kernel, us, vmem=VMEM, **kwargs):
     cost = pl.CostEstimate(flops=int(us * 1e9), bytes_accessed=1024, transcendentals=0)
-    params = pltpu.CompilerParams(vmem_limit_bytes=VMEM)
+    params = pltpu.CompilerParams(vmem_limit_bytes=vmem)
     return pl.pallas_call(kernel, cost_estimate=cost, compiler_params=params, **kwargs)
 
 
@@ -462,11 +467,11 @@
         pltpu.VMEM((D, 3 * D), bf16),
         pltpu.VMEM((D, D), bf16),
         pltpu.VMEM((GROUPS, CTOK, QUAD), bf16),
-        pltpu.VMEM((GROUPS, 3, CTOK, QUAD), bf16),
+        pltpu.VMEM((GROUPS, CTOK, 3 * QUAD), bf16),
     ]
 
 
-ATT, ROWSET = (GROUPS, CTOK, QUAD), (GROUPS, 3, CTOK, QUAD)
+ATT, ROWSET = (GROUPS, CTOK, QUAD), (GROUPS, CTOK, 3 * QUAD)
 
 
 def first_chunk(up, lo, qkv_weight, out_weight):
@@ -491,16 +496,17 @@
 def second_chunk(core, upa, loa, up, lo, eup, elo, qkv_weight, out_weight, att, rows):
     by_lon, out_by_lon = jnp.asarray(BY_LON, bf16), jnp.asarray(OUT_BY_LON, bf16)
     ready = (LONS // 2, READY, D)
+    ret, rim = (2, PACKED - SPLIT, D), (2, RIMP, D)
     return call(
         chunk_b_kernel,
         18,
         in_specs=[pl.BlockSpec(memory_space=pltpu.SMEM)] + anywhere(12),
-        out_specs=anywhere(4),
-        out_shape=[shaped(*o) for o in (ATT, ROWSET, ready, ready)],
+        out_specs=anywhere(6),
+        out_shape=[shaped(*o) for o in (ready, ready, ret, ret, rim, rim)],
         scratch_shapes=[
             *common(),
             pltpu.SemaphoreType.DMA((4 * (CHUNK - 1) + 7,)),
-            pltpu.SemaphoreType.DMA((2 * GROUPS + 2,)),
+            pltpu.SemaphoreType.DMA((6,)),
             pltpu.SemaphoreType.DMA((4 * CHUNK + 4,)),
             pltpu.VMEM((2, 2, RIMP, D), bf16),
             pltpu.VMEM((2, 2, RIMP, D), bf16),
@@ -511,9 +517,22 @@
             pltpu.VMEM(by_lon.shape[1:], bf16),
             pltpu.VMEM(out_by_lon.shape[1:], bf16),
             pltpu.VMEM((2, *ready), bf16),
+            pltpu.VMEM(ret, bf16),
+            pltpu.VMEM(ret, bf16),
+            pltpu.VMEM(rim, bf16),
+            pltpu.VMEM(rim, bf16),
             *scratches(),
         ],
     )(core, upa, loa, up, lo, eup, elo, qkv_weight, out_weight, att, rows, by_lon, out_by_lon)
+
+
+def groups_of(*keys):
+    groups = {}
+    for i in range(LATS):
+        for j in range(LONS):
+            parts = split(i, j)
+            groups.setdefault(tuple(parts[k] for k in keys), []).append(i * LONS + j)
+    return list(groups.values())
 
 
 def other_core(i, j):
@@ -550,19 +569,14 @@
     atta, rowsa, rupa, rloa = first_chunk(upa, loa, *weights)
     atta, rupa, rloa = lax.optimization_barrier((atta, rupa, rloa))
     rupa, rloa = unsend(rupa, to_upper), unsend(rloa, to_lower)
-    attb, rowsb, mine, theirs = second_chunk(
+    mine, theirs, rupb, rlob, reup, relo = second_chunk(
         core, upa, loa, upb, lob, eup, elo, *weights, atta, rowsa
     )
-    attb, mine, theirs, rupa, rloa = lax.optimization_barrier((attb, mine, theirs, rupa, rloa))
+    rupb, theirs, rupa, rloa = lax.optimization_barrier((rupb, theirs, rupa, rloa))
     theirs = send(theirs, other_core)
-
-    rupb, rlob, reup, relo = call(
-        back_b_kernel, 4, out_shape=[shaped(*s) for s in (b, b, edge, edge)]
-    )(attb, rowsb, *weights)
+    theirs, rupb, rlob = lax.optimization_barrier((theirs, rupb, rlob))
     ready = (mine.astype(f32) + theirs.astype(f32)).astype(bf16)
-    ready, rupb, rlob, reup, relo = lax.optimization_barrier((ready, rupb, rlob, reup, relo))
-    cores = [list(range(i, LONS, 2)) for i in range(2)]
-    parts = lax.all_to_all(ready, "lon", 0, 0, axis_index_groups=cores)
+    parts = lax.all_to_all(ready, ("lat", "lon"), 0, 0, axis_index_groups=groups_of(0, 2))
     rupb, rlob = unsend(rupb, to_upper), unsend(rlob, to_lower)
     reup, relo = unsend(reup, to_upper_rim), unsend(relo, to_lower_rim)
     half = pl.BlockSpec((LEV, SHIFT, COLS, D), lambda i: (0, i, 0, 0))
@@ -570,16 +584,24 @@
     output, grad_features = call(
         behind_kernel,
         6,
+        MOST,
         grid=(2,),
         in_specs=[half, half] + [fixed(r.shape) for r in returned],
         out_specs=[half, half],
         out_shape=[shaped(*features.shape)] * 2,
     )(features, grad_output, *returned)
 
-    by_lat = jnp.asarray(BY_LAT, bf16)[lax.axis_index("lon")]
-    part = call(sum_kernel, 2, out_shape=shaped(LATS, 8, D))(parts, by_lat)
-    part = lax.all_to_all(part, "lat", 0, 0).astype(f32).sum(0)
-    return (output, grad_features, part[:SPAN].T, part[SPAN:].T)
+    lat, lon = lax.axis_index("lat"), lax.axis_index("lon")
+    by_lat = jnp.asarray(BY_LAT, bf16)[lon % 2 * LONS // 2 + lat // 2 % 2 * 4 + lon // 4]
+    part = call(sum_kernel, 2, MOST, out_shape=shaped(LATS, 8, D))(parts, by_lat)
+    part = lax.all_to_all(part, ("lat", "lon"), 0, 0, axis_index_groups=groups_of(0, 1))
+    grad_qkv, grad_out = call(
+        last_kernel,
+        1,
+        MOST,
+        out_shape=[shaped(SPAN, D, dtype=f32), shaped(SPAN_OUT, D, dtype=f32)],
+    )(part)
+    return (output, grad_features, grad_qkv.T, grad_out.T)
 
 
 def solution(mesh):

time: 123 us -> 119 us (0.967)
  Pallas kernels: 56.5 us -> 53.2 us
  local copies, waits for them, and re-layouts: 6.87 us -> 3.8 us
  starting transfers between devices: 43.5 us -> 45.6 us
  waiting for transfers between devices: 12.8 us -> 10.8 us
    ppermute x7, waiting for transfers between devices: 0.02 us -> 4.4 us  [send(): return lax.ppermute(x, ('lat', 'lon'), pairs)]
    all_to_all x2, waiting for transfers between devices: 8.11 us -> 4.25 us  [the longest x1 3.81 us: shards(): lax.all_to_all(ready, ('lat', 'lon'), 0, 0, axis_index_groups=groups_of(0...]
    pallas_call x3, Pallas kernels: 13.8 us -> 10.5 us  [the longest x1 6.76 us: shards(): call(behind_kernel, 6, MOST, grid=(2,), in_specs=[half, half] + [fixed(r....]
    ppermute x6, starting transfers between devices: 9.07 us -> 12.1 us  [unsend(): return lax.ppermute(x, ('lat', 'lon'), pairs)]
    ppermute x6, waiting for transfers between devices: 4.69 us -> 2.11 us  [unsend(): return lax.ppermute(x, ('lat', 'lon'), pairs)]
    unnamed x34 -> x22, local copies, waits for them, and re-layouts: 4.3 us -> 2.42 us
    ppermute x7, starting transfers between devices: 25.2 us -> 23.7 us  [send(): return lax.ppermute(x, ('lat', 'lon'), pairs)]
  transfers between devices with their start and end apart: 15 -> 15, of which waited for: 2 -> 5; matrix products, arithmetic and copies ran while one was open for 1% -> 1% of each run, Pallas kernels for 43% -> 41%
where the time goes in v2:
time: 119 us; the launch traced here: 117 us
  Pallas kernels  53.2 us (45%)
  starting transfers between devices  45.6 us (38%)
  waiting for transfers between devices  10.8 us (9%)
  local copies, waits for them, and re-layouts  3.8 us (3%)
  other arithmetic  2.5 us (2%)
    ppermute x7, starting transfers between devices, send(): return lax.ppermute(x, ('lat', 'lon'), pairs)  23.7 us
    pallas_call x1, Pallas kernels, second_chunk(): call(chunk_b_kernel, 18, in_specs=[pl.BlockSpec(memory_space=pltpu.SMEM)]...  21 us
    pallas_call x1, Pallas kernels, first_chunk(): call(chunk_a_kernel, 13, in_specs=anywhere(4), out_specs=anywhere(4), out...  13.6 us
    ppermute x6, starting transfers between devices, unsend(): return lax.ppermute(x, ('lat', 'lon'), pairs)  12.1 us
    pallas_call x1, Pallas kernels, shards(): call(behind_kernel, 6, MOST, grid=(2,), in_specs=[half, half] + [fixed(r....  6.76 us
    all_to_all x1, starting transfers between devices, shards(): lax.all_to_all(part, ('lat', 'lon'), 0, 0, axis_index_groups=groups_of(0,...  5.36 us
    ppermute x7, waiting for transfers between devices, send(): return lax.ppermute(x, ('lat', 'lon'), pairs)  4.4 us
    pallas_call x1, Pallas kernels, shards(): call(late_kernel, 5, out_shape=[shaped(*s) for s in (b, b, edge, edge)],...  4.4 us
  transfers between devices with their start and end apart: 15, of which 5 were waited for; matrix products, arithmetic and copies ran while one was open for 1% of the time, Pallas kernels for 41%

profile of v2, /device:TPU:1, one launch (start us, length us, event | category | flops | bytes accessed | tf_op | source)
XLA Modules:
  0.0 116.6 jit_solution(12840271352914254566)
XLA Ops:
  0.6 3.7 %shard_map.147 = (bf16[2,304,512]{2,1,0:T(8,128)(2,1)}, bf16[2,288,512]{2,1,0:T(8,128)(2,1)}) custom-call(bf16[2,12,48,512]{3,2,1,0:T(8,128)(2,1)} %x_ref.3, bf16[2,12,48,512]{3,2,1,0:T(8,128)(2,1)} %g_ref.3, s32[12,48]{1,0:T(8,128)} %regions_ref.1, bf16[288,384]{1,0:T(8,128)(2,1)} %constant.74.clone.place_ref), custom_call_target="tpu_custom_call" | custom-call | flops 3000000000 | bytes 1024 | tf_op jit(solution)/shard_map/pallas_call | solution.py:548
  4.3 3.6 %collective-permute-start = (bf16[2,304,512]{2,1,0:T(8,128)(2,1)}, bf16[2,304,512]{2,1,0:T(8,128)(2,1)S(1)}, u32[]{:S(2)}, u32[]{:S(2)}) collective-permute-start(bf16[2,304,512]{2,1,0:T(8,128)(2,1)} %get-tuple-element.42), channel_id=1, source_target_pairs={{0,16},{1,17},{2,18},{3,19},{4,20},{5,21},{6,22},{7,23},{8,24},{9,... | collective-permute-start | bytes 1867784 | tf_op jit(solution)/shard_map/ppermute | solution.py:402
  7.9 7.5 %collective-permute-start.1 = (bf16[2,288,512]{2,1,0:T(8,128)(2,1)}, bf16[2,288,512]{2,1,0:T(8,128)(2,1)S(1)}, u32[]{:S(2)}, u32[]{:S(2)}) collective-permute-start(bf16[2,288,512]{2,1,0:T(8,128)(2,1)} %get-tuple-element.43), channel_id=1, source_target_pairs={{0,224},{1,225},{2,226},{3,227},{4,228},{5,229},{6,230},{7,231},{8... | collective-permute-start | bytes 1769480 | tf_op jit(solution)/shard_map/ppermute | solution.py:402
  15.4 4.4 %shard_map.148 = (bf16[2,224,512]{2,1,0:T(8,128)(2,1)}, bf16[2,224,512]{2,1,0:T(8,128)(2,1)}, bf16[2,80,512]{2,1,0:T(8,128)(2,1)}, bf16[2,80,512]{2,1,0:T(8,128)(2,1)}) custom-call(bf16[2,12,48,512]{3,2,1,0:T(8,128)(2,1)} %x_ref.3, bf16[2,12,48,512]{3,2,1,0:T(8,128)(2,1)} %g_ref.3, bf16[224,576]{1,0:T(8,128)(2,1)} %constant.75.clone.place_ref, ...), custom_call_target="tpu_custom_call" | custom-call | flops 5000000000 | bytes 1024 | tf_op jit(solution)/shard_map/pallas_call | solution.py:559
  19.8 0.0 collective-permute-start.2
  19.8 2.6 %collective-permute-start.3 = (bf16[2,224,512]{2,1,0:T(8,128)(2,1)}, bf16[2,224,512]{2,1,0:T(8,128)(2,1)S(1)}, u32[]{:S(2)}, u32[]{:S(2)}) collective-permute-start(bf16[2,224,512]{2,1,0:T(8,128)(2,1)} %get-tuple-element.45), channel_id=1, source_target_pairs={{0,224},{1,225},{2,226},{3,227},{4,228},{5,229},{6,230},{7,231},{8... | collective-permute-start | bytes 1376264 | tf_op jit(solution)/shard_map/ppermute | solution.py:402
  22.4 3.4 %collective-permute-start.4 = (bf16[2,80,512]{2,1,0:T(8,128)(2,1)}, bf16[2,80,512]{2,1,0:T(8,128)(2,1)S(1)}, u32[]{:S(2)}, u32[]{:S(2)}) collective-permute-start(bf16[2,80,512]{2,1,0:T(8,128)(2,1)} %get-tuple-element.46), channel_id=1, source_target_pairs={{0,31},{1,16},{2,17},{3,18},{4,19},{5,20},{6,21},{7,22},{8,23},{9,... | collective-permute-start | bytes 491528 | tf_op jit(solution)/shard_map/ppermute | solution.py:402
  25.8 1.5 %collective-permute-done.1.lo.loa = bf16[2,288,512]{2,1,0:T(8,128)(2,1)S(1)} collective-permute-done((bf16[2,288,512]{2,1,0:T(8,128)(2,1)}, bf16[2,288,512]{2,1,0:T(8,128)(2,1)S(1)}, u32[]{:S(2)}, u32[]{:S(2)}) %collective-permute-start.1) | collective-permute-done | bytes 589856 | tf_op jit(solution)/shard_map/ppermute | solution.py:402
  27.3 0.0 copy-start.4
  27.3 6.5 %collective-permute-start.5 = (bf16[2,80,512]{2,1,0:T(8,128)(2,1)}, bf16[2,80,512]{2,1,0:T(8,128)(2,1)S(1)}, u32[]{:S(2)}, u32[]{:S(2)}) collective-permute-start(bf16[2,80,512]{2,1,0:T(8,128)(2,1)} %get-tuple-element.47), channel_id=1, source_target_pairs={{0,239},{1,224},{2,225},{3,226},{4,227},{5,228},{6,229},{7,230},{8... | collective-permute-start | bytes 491528 | tf_op jit(solution)/shard_map/ppermute | solution.py:402
  33.9 0.0 collective-permute-done.up.upa
  33.9 0.0 copy-done.4
  33.9 0.0 copy-start.1
  33.9 0.8 copy-done.1
  34.7 13.6 %shard_map.149 = (bf16[2,576,256]{2,1,0:T(8,128)(2,1)}, bf16[2,576,768]{2,1,0:T(8,128)(2,1)}, bf16[2,288,512]{2,1,0:T(8,128)(2,1)}, bf16[2,288,512]{2,1,0:T(8,128)(2,1)}) custom-call(bf16[2,304,512]{2,1,0:T(8,128)(2,1)} %copy-done.1, bf16[2,288,512]{2,1,0:T(8,128)(2,1)} %copy-done.4, bf16[512,1536]{1,0:T(8,128)(2,1)} %wqkv.3, bf16[512,512]{1,0:T(8,128)(2,1)} %wout.3), custom_call_target="tpu_custom_call" | custom-call | flops 12999999488 | bytes 1024 | tf_op jit(solution)/shard_map/pallas_call | solution.py:479
  48.3 0.1 collective-permute-start.6
  48.4 0.0 collective-permute-done.4.eup
  48.4 0.0 copy-start.9
  48.5 2.1 %collective-permute-start.7 = (bf16[2,288,512]{2,1,0:T(8,128)(2,1)}, bf16[2,288,512]{2,1,0:T(8,128)(2,1)S(1)}, u32[]{:S(2)}, u32[]{:S(2)}) collective-permute-start(bf16[2,288,512]{2,1,0:T(8,128)(2,1)} %get-tuple-element.56), channel_id=1, source_target_pairs={{224,0},{225,1},{226,2},{227,3},{228,4},{229,5},{230,6},{231,7},{2... | collective-permute-start | bytes 1769480 | tf_op jit(solution)/shard_map/ppermute | solution.py:411
  50.6 0.0 collective-permute-done.5.elo
  50.6 0.0 copy-start.10
  50.6 0.0 collective-permute-done.2.up
  50.6 0.0 copy-start.5
  50.6 0.0 collective-permute-done.3.lo
  50.7 0.0 copy-start.6
  50.7 0.0 copy-done.9
  50.7 0.6 copy-done.10
  51.3 0.2 copy-done.5
  51.5 0.1 copy-done.6
  51.6 21.0 %shard_map.150 = (bf16[8,128,512]{2,1,0:T(8,128)(2,1)}, bf16[8,128,512]{2,1,0:T(8,128)(2,1)}, bf16[2,224,512]{2,1,0:T(8,128)(2,1)}, bf16[2,224,512]{2,1,0:T(8,12...) custom-call(s32[1]{0:T(128)} %bitcast.core_ref, bf16[2,304,512]{2,1,0:T(8,128)(2,1)} %copy-done.1, ...), custom_call_target="tpu_custom_call" | custom-call | flops 17999998976 | bytes 1024 | tf_op jit(solution)/shard_map/pallas_call | solution.py:500
  72.6 0.0 collective-permute-done.6.upa_ref
  72.6 0.0 copy-start.2
  72.6 0.0 collective-permute-done.7.loa_ref
  72.6 0.0 copy-start.3
  72.6 0.1 collective-permute-start.8
  72.7 2.9 %collective-permute-done.8 = bf16[8,128,512]{2,1,0:T(8,128)(2,1)S(1)} collective-permute-done((bf16[8,128,512]{2,1,0:T(8,128)(2,1)}, bf16[8,128,512]{2,1,0:T(8,128)(2,1)S(1)}, u32[]{:S(2)}, u32[]{:S(2)}) %collective-permute-start.8) | collective-permute-done | bytes 1048608 | tf_op jit(solution)/shard_map/ppermute | solution.py:402
  75.6 0.0 copy-done.2
  75.6 2.5 %add_convert_fusion = bf16[8,128,512]{2,1,0:T(8,128)(2,1)} fusion(bf16[8,128,512]{2,1,0:T(8,128)(2,1)S(1)} %collective-permute-done.8, bf16[8,128,512]{2,1,0:T(8,128)(2,1)} %get-tuple-element.68), kind=kLoop, calls=%fused_computation | loop fusion | flops 2097152 | bytes 3145728 | tf_op jit(solution)/shard_map/convert_element_type | solution.py:578
  78.1 0.0 copy-start.8
  78.1 0.0 copy-start.7
  78.1 0.0 copy-done.3
  78.1 4.4 %all-to-all-start = ((bf16[8,128,512]{2,1,0:T(8,128)(2,1)}), bf16[8,128,512]{2,1,0:T(8,128)(2,1)}, u32[]{:S(2)}, u32[]{:S(2)}) async-start(bf16[8,128,512]{2,1,0:T(8,128)(2,1)} %add_convert_fusion), calls=%async_computation | async-start | bytes 2097152 | tf_op jit(solution)/shard_map/all_to_all | solution.py:579
  82.5 3.3 %collective-permute-start.10 = (bf16[2,224,512]{2,1,0:T(8,128)(2,1)}, bf16[2,224,512]{2,1,0:T(8,128)(2,1)}, u32[]{:S(2)}, u32[]{:S(2)}) collective-permute-start(bf16[2,224,512]{2,1,0:T(8,128)(2,1)} %get-tuple-element.63), channel_id=1, source_target_pairs={{224,0},{225,1},{226,2},{227,3},{228,4},{229,5},{230,6},{231,7},{2... | collective-permute-start | bytes 1376264 | tf_op jit(solution)/shard_map/ppermute | solution.py:411
  85.8 4.3 %collective-permute-start.9 = (bf16[2,224,512]{2,1,0:T(8,128)(2,1)}, bf16[2,224,512]{2,1,0:T(8,128)(2,1)}, u32[]{:S(2)}, u32[]{:S(2)}) collective-permute-start(bf16[2,224,512]{2,1,0:T(8,128)(2,1)} %get-tuple-element.62), channel_id=1, source_target_pairs={{16,0},{17,1},{18,2},{19,3},{20,4},{21,5},{22,6},{23,7},{24,8},{25... | collective-permute-start | bytes 1376264 | tf_op jit(solution)/shard_map/ppermute | solution.py:411
  90.0 1.4 %dynamic-slice_bitcast_fusion.by_ref = bf16[128,128]{1,0:T(8,128)(2,1)} fusion(bf16[16,128,128]{2,1,0:T(8,128)(2,1)} %constant.78.clone, s32[]{:T(128)S(6)} %select_n.31), kind=kLoop, calls=%fused_computation.1 | loop fusion | bytes 65540 | tf_op jit(solution)/shard_map/squeeze | solution.py:595
  91.4 0.0 copy-done.8
  91.4 0.0 collective-permute-start.11
  91.4 0.0 copy-done.7
  91.4 2.4 %collective-permute-start.12 = (bf16[2,80,512]{2,1,0:T(8,128)(2,1)S(1)}, bf16[2,80,512]{2,1,0:T(8,128)(2,1)}, u32[]{:S(2)}, u32[]{:S(2)}) collective-permute-start(bf16[2,80,512]{2,1,0:T(8,128)(2,1)S(1)} %copy-done.7), channel_id=1, source_target_pairs={{239,0},{224,1},{225,2},{226,3},{227,4},{228,5},{229,6},{230,7},{2... | collective-permute-start | bytes 491528 | tf_op jit(solution)/shard_map/ppermute | solution.py:411
  93.8 3.8 %all-to-all-done.parts_ref = bf16[8,128,512]{2,1,0:T(8,128)(2,1)} async-done(((bf16[8,128,512]{2,1,0:T(8,128)(2,1)}), bf16[8,128,512]{2,1,0:T(8,128)(2,1)}, u32[]{:S(2)}, u32[]{:S(2)}) %all-to-all-start) | async-done | bytes 1048608 | tf_op jit(solution)/shard_map/all_to_all | solution.py:579
  97.6 2.2 %shard_map.152 = bf16[16,8,512]{2,1,0:T(8,128)(2,1)} custom-call(bf16[8,128,512]{2,1,0:T(8,128)(2,1)} %all-to-all-done.parts_ref, bf16[128,128]{1,0:T(8,128)(2,1)} %dynamic-slice_bitcast_fusion.by_ref), custom_call_target="tpu_custom_call" | custom-call | flops 2000000000 | bytes 1024 | tf_op jit(solution)/shard_map/pallas_call | solution.py:596
  99.8 5.4 %all-to-all-start.1 = ((bf16[16,8,512]{2,1,0:T(8,128)(2,1)}), bf16[16,8,512]{2,1,0:T(8,128)(2,1)S(1)}, u32[]{:S(2)}, u32[]{:S(2)}) async-start(bf16[16,8,512]{2,1,0:T(8,128)(2,1)} %shard_map.152), calls=%async_computation.1 | async-start | bytes 262144 | tf_op jit(solution)/shard_map/all_to_all | solution.py:597
  105.1 0.0 collective-permute-done.11.eup_ref
  105.1 2.1 %collective-permute-done.12.elo_ref = bf16[2,80,512]{2,1,0:T(8,128)(2,1)} collective-permute-done((bf16[2,80,512]{2,1,0:T(8,128)(2,1)S(1)}, bf16[2,80,512]{2,1,0:T(8,128)(2,1)}, u32[]{:S(2)}, u32[]{:S(2)}) %collective-permute-start.12) | collective-permute-done | bytes 163872 | tf_op jit(solution)/shard_map/ppermute | solution.py:411
  107.2 0.0 collective-permute-done.10.lob_ref
  107.2 0.0 collective-permute-done.9.upb_ref
  107.2 6.8 %shard_map.151 = (bf16[2,12,48,512]{3,2,1,0:T(8,128)(2,1)}, bf16[2,12,48,512]{3,2,1,0:T(8,128)(2,1)}) custom-call(bf16[2,12,48,512]{3,2,1,0:T(8,128)(2,1)} %x_ref.3, bf16[2,12,48,512]{3,2,1,0:T(8,128)(2,1)} %g_ref.3, bf16[2,288,512]{2,1,0:T(8,128)(2,1)} %copy-done.2, bf16[2,288,512]{2,1,0:T(8,128)(2,1)} %copy-done.3, ...), custom_call_target="tpu_custom_call" | custom-call | flops 6000000000 | bytes 1024 | tf_op jit(solution)/shard_map/pallas_call | solution.py:584
  114.0 0.4 all-to-all-done.1.parts_ref
  114.5 0.0 copy-start
  114.5 0.6 copy-done
  115.1 1.5 %shard_map.153 = (f32[6,512]{1,0:T(8,128)}, f32[2,512]{1,0:T(2,128)}) custom-call(bf16[16,8,512]{2,1,0:T(8,128)(2,1)} %copy-done), custom_call_target="tpu_custom_call" | custom-call | flops 1000000000 | bytes 1024 | tf_op jit(solution)/shard_map/pallas_call | solution.py:598
Async XLA Ops:
  4.3 29.6 %collective-permute-start = (bf16[2,304,512]{2,1,0:T(8,128)(2,1)}, bf16[2,304,512]{2,1,0:T(8,128)(2,1)S(1)}, u32[]{:S(2)}, u32[]{:S(2)}) collective-permute-start(bf16[2,304,512]{2,1,0:T(8,128)(2,1)} %get-tuple-element.42), channel_id=1, source_target_pairs={{0,16},{1,17},{2,18},{3,19},{4,20},{5,21},{6,22},{7,23},{8,24},{9,... | collective-permute-start | bytes 1867784 | tf_op jit(solution)/shard_map/ppermute | solution.py:402
  7.9 19.4 %collective-permute-start.1 = (bf16[2,288,512]{2,1,0:T(8,128)(2,1)}, bf16[2,288,512]{2,1,0:T(8,128)(2,1)S(1)}, u32[]{:S(2)}, u32[]{:S(2)}) collective-permute-start(bf16[2,288,512]{2,1,0:T(8,128)(2,1)} %get-tuple-element.43), channel_id=1, source_target_pairs={{0,224},{1,225},{2,226},{3,227},{4,228},{5,229},{6,230},{7,231},{8... | collective-permute-start | bytes 1769480 | tf_op jit(solution)/shard_map/ppermute | solution.py:402
  19.8 30.9 %collective-permute-start.2 = (bf16[2,224,512]{2,1,0:T(8,128)(2,1)}, bf16[2,224,512]{2,1,0:T(8,128)(2,1)S(1)}, u32[]{:S(2)}, u32[]{:S(2)}) collective-permute-start(bf16[2,224,512]{2,1,0:T(8,128)(2,1)} %get-tuple-element.44), channel_id=1, source_target_pairs={{0,16},{1,17},{2,18},{3,19},{4,20},{5,21},{6,22},{7,23},{8,24},{9,... | collective-permute-start | bytes 1376264 | tf_op jit(solution)/shard_map/ppermute | solution.py:402
  19.8 30.9 %collective-permute-start.3 = (bf16[2,224,512]{2,1,0:T(8,128)(2,1)}, bf16[2,224,512]{2,1,0:T(8,128)(2,1)S(1)}, u32[]{:S(2)}, u32[]{:S(2)}) collective-permute-start(bf16[2,224,512]{2,1,0:T(8,128)(2,1)} %get-tuple-element.45), channel_id=1, source_target_pairs={{0,224},{1,225},{2,226},{3,227},{4,228},{5,229},{6,230},{7,231},{8... | collective-permute-start | bytes 1376264 | tf_op jit(solution)/shard_map/ppermute | solution.py:402
  22.4 26.0 %collective-permute-start.4 = (bf16[2,80,512]{2,1,0:T(8,128)(2,1)}, bf16[2,80,512]{2,1,0:T(8,128)(2,1)S(1)}, u32[]{:S(2)}, u32[]{:S(2)}) collective-permute-start(bf16[2,80,512]{2,1,0:T(8,128)(2,1)} %get-tuple-element.46), channel_id=1, source_target_pairs={{0,31},{1,16},{2,17},{3,18},{4,19},{5,20},{6,21},{7,22},{8,23},{9,... | collective-permute-start | bytes 491528 | tf_op jit(solution)/shard_map/ppermute | solution.py:402
  27.3 6.5 %copy-start.4 = (bf16[2,288,512]{2,1,0:T(8,128)(2,1)}, bf16[2,288,512]{2,1,0:T(8,128)(2,1)S(1)}, u32[]{:S(2)}) copy-start(bf16[2,288,512]{2,1,0:T(8,128)(2,1)S(1)} %collective-permute-done.1.lo.loa) | copy-start | bytes 1769476
  27.3 23.3 %collective-permute-start.5 = (bf16[2,80,512]{2,1,0:T(8,128)(2,1)}, bf16[2,80,512]{2,1,0:T(8,128)(2,1)S(1)}, u32[]{:S(2)}, u32[]{:S(2)}) collective-permute-start(bf16[2,80,512]{2,1,0:T(8,128)(2,1)} %get-tuple-element.47), channel_id=1, source_target_pairs={{0,239},{1,224},{2,225},{3,226},{4,227},{5,228},{6,229},{7,230},{8... | collective-permute-start | bytes 491528 | tf_op jit(solution)/shard_map/ppermute | solution.py:402
  33.9 0.8 copy-start.1
  48.3 24.3 %collective-permute-start.6 = (bf16[2,288,512]{2,1,0:T(8,128)(2,1)}, bf16[2,288,512]{2,1,0:T(8,128)(2,1)S(1)}, u32[]{:S(2)}, u32[]{:S(2)}) collective-permute-start(bf16[2,288,512]{2,1,0:T(8,128)(2,1)} %get-tuple-element.55), channel_id=1, source_target_pairs={{16,0},{17,1},{18,2},{19,3},{20,4},{21,5},{22,6},{23,7},{24,8},{25... | collective-permute-start | bytes 1769480 | tf_op jit(solution)/shard_map/ppermute | solution.py:411
  48.4 2.2 %copy-start.9 = (bf16[2,80,512]{2,1,0:T(8,128)(2,1)}, bf16[2,80,512]{2,1,0:T(8,128)(2,1)S(1)}, u32[]{:S(2)}) copy-start(bf16[2,80,512]{2,1,0:T(8,128)(2,1)S(1)} %collective-permute-done.4.eup) | copy-start | bytes 491524
  48.5 24.2 %collective-permute-start.7 = (bf16[2,288,512]{2,1,0:T(8,128)(2,1)}, bf16[2,288,512]{2,1,0:T(8,128)(2,1)S(1)}, u32[]{:S(2)}, u32[]{:S(2)}) collective-permute-start(bf16[2,288,512]{2,1,0:T(8,128)(2,1)} %get-tuple-element.56), channel_id=1, source_target_pairs={{224,0},{225,1},{226,2},{227,3},{228,4},{229,5},{230,6},{231,7},{2... | collective-permute-start | bytes 1769480 | tf_op jit(solution)/shard_map/ppermute | solution.py:411
  50.6 0.7 copy-start.10
  50.6 0.8 copy-start.5
  50.7 0.9 copy-start.6
  72.6 3.0 %copy-start.2 = (bf16[2,288,512]{2,1,0:T(8,128)(2,1)}, bf16[2,288,512]{2,1,0:T(8,128)(2,1)S(1)}, u32[]{:S(2)}) copy-start(bf16[2,288,512]{2,1,0:T(8,128)(2,1)S(1)} %collective-permute-done.6.upa_ref) | copy-start | bytes 1769476
  72.6 5.5 %copy-start.3 = (bf16[2,288,512]{2,1,0:T(8,128)(2,1)}, bf16[2,288,512]{2,1,0:T(8,128)(2,1)S(1)}, u32[]{:S(2)}) copy-start(bf16[2,288,512]{2,1,0:T(8,128)(2,1)S(1)} %collective-permute-done.7.loa_ref) | copy-start | bytes 1769476
  72.6 3.0 %collective-permute-start.8 = (bf16[8,128,512]{2,1,0:T(8,128)(2,1)}, bf16[8,128,512]{2,1,0:T(8,128)(2,1)S(1)}, u32[]{:S(2)}, u32[]{:S(2)}) collective-permute-start(bf16[8,128,512]{2,1,0:T(8,128)(2,1)} %get-tuple-element.59), channel_id=1, source_target_pairs={{0,1},{1,0},{2,3},{3,2},{4,5},{5,4},{6,7},{7,6},{8,9},{9,8},{10,11... | collective-permute-start | bytes 3145736 | tf_op jit(solution)/shard_map/ppermute | solution.py:402
  78.1 13.3 %copy-start.8 = (bf16[2,80,512]{2,1,0:T(8,128)(2,1)S(1)}, bf16[2,80,512]{2,1,0:T(8,128)(2,1)}, u32[]{:S(2)}) copy-start(bf16[2,80,512]{2,1,0:T(8,128)(2,1)} %get-tuple-element.64) | copy-start | bytes 491524
  78.1 13.3 %copy-start.7 = (bf16[2,80,512]{2,1,0:T(8,128)(2,1)S(1)}, bf16[2,80,512]{2,1,0:T(8,128)(2,1)}, u32[]{:S(2)}) copy-start(bf16[2,80,512]{2,1,0:T(8,128)(2,1)} %get-tuple-element.65) | copy-start | bytes 491524
  78.1 19.5 %all-to-all-start = ((bf16[8,128,512]{2,1,0:T(8,128)(2,1)}), bf16[8,128,512]{2,1,0:T(8,128)(2,1)}, u32[]{:S(2)}, u32[]{:S(2)}) async-start(bf16[8,128,512]{2,1,0:T(8,128)(2,1)} %add_convert_fusion), calls=%async_computation | async-start | bytes 2097152 | tf_op jit(solution)/shard_map/all_to_all | solution.py:579
  82.5 24.8 %collective-permute-start.10 = (bf16[2,224,512]{2,1,0:T(8,128)(2,1)}, bf16[2,224,512]{2,1,0:T(8,128)(2,1)}, u32[]{:S(2)}, u32[]{:S(2)}) collective-permute-start(bf16[2,224,512]{2,1,0:T(8,128)(2,1)} %get-tuple-element.63), channel_id=1, source_target_pairs={{224,0},{225,1},{226,2},{227,3},{228,4},{229,5},{230,6},{231,7},{2... | collective-permute-start | bytes 1376264 | tf_op jit(solution)/shard_map/ppermute | solution.py:411
  85.8 21.5 %collective-permute-start.9 = (bf16[2,224,512]{2,1,0:T(8,128)(2,1)}, bf16[2,224,512]{2,1,0:T(8,128)(2,1)}, u32[]{:S(2)}, u32[]{:S(2)}) collective-permute-start(bf16[2,224,512]{2,1,0:T(8,128)(2,1)} %get-tuple-element.62), channel_id=1, source_target_pairs={{16,0},{17,1},{18,2},{19,3},{20,4},{21,5},{22,6},{23,7},{24,8},{25... | collective-permute-start | bytes 1376264 | tf_op jit(solution)/shard_map/ppermute | solution.py:411
  91.4 13.7 %collective-permute-start.11 = (bf16[2,80,512]{2,1,0:T(8,128)(2,1)S(1)}, bf16[2,80,512]{2,1,0:T(8,128)(2,1)}, u32[]{:S(2)}, u32[]{:S(2)}) collective-permute-start(bf16[2,80,512]{2,1,0:T(8,128)(2,1)S(1)} %copy-done.8), channel_id=1, source_target_pairs={{31,0},{16,1},{17,2},{18,3},{19,4},{20,5},{21,6},{22,7},{23,8},{24... | collective-permute-start | bytes 491528 | tf_op jit(solution)/shard_map/ppermute | solution.py:411
  91.4 15.8 %collective-permute-start.12 = (bf16[2,80,512]{2,1,0:T(8,128)(2,1)S(1)}, bf16[2,80,512]{2,1,0:T(8,128)(2,1)}, u32[]{:S(2)}, u32[]{:S(2)}) collective-permute-start(bf16[2,80,512]{2,1,0:T(8,128)(2,1)S(1)} %copy-done.7), channel_id=1, source_target_pairs={{239,0},{224,1},{225,2},{226,3},{227,4},{228,5},{229,6},{230,7},{2... | collective-permute-start | bytes 491528 | tf_op jit(solution)/shard_map/ppermute | solution.py:411
  99.8 14.7 %all-to-all-start.1 = ((bf16[16,8,512]{2,1,0:T(8,128)(2,1)}), bf16[16,8,512]{2,1,0:T(8,128)(2,1)S(1)}, u32[]{:S(2)}, u32[]{:S(2)}) async-start(bf16[16,8,512]{2,1,0:T(8,128)(2,1)} %shard_map.152), calls=%async_computation.1 | async-start | bytes 262144 | tf_op jit(solution)/shard_map/all_to_all | solution.py:597
  114.5 0.7 copy-start
